TPU v7x, 512 devices: a whole 4x4x16 slice. The times are simulated.
512 devices in a mesh: wave: 128 (over x, z, core), basin: 4 (over y).
Axes of the slice: x: 4, y: 4, z: 16, core: 2. Of those that a mesh axis runs over, the one named last changes fastest.
Arguments:
- spectra: bfloat16 [16, 2, 1280, 1280], P('basin', None, 'wave'), may hold values from -6 to 6
- legendre: bfloat16 [1280, 1280, 128], P('wave'), may hold values from -0.15625 to 0.15625
- wave_numbers: int32 [1280], P('wave'), may hold values from 0 to 1279, each once
- block_index: int32 [128, 1024], P('wave'), may hold values from 0 to 159
- block_weights: bfloat16 [128, 1024, 128], P('wave'), may hold values from 0.019897461 to 0.19921875
- basin_index: int32 [128, 1024], P('wave'), may hold values from 0 to 65535, as said below
Outputs:
- grid_fields: bfloat16 [16, 2, 128, 10240], P('basin', None, 'wave')
- basin_sums: float32 [16, 65536], P(None, ('wave', 'basin'))
Inputs may be any that keep to these rules, and one draw needn't show every extreme that they name: `basin_index`: the owner of basin b along wave is b // 512; the 1024 rows of one latitude pair name basins of exactly 64 owners, 16 rows for each.
All inputs are finite; a program needn't handle non-finite values.
Results may differ from a plain program's by a relative error of at most 0.0061.
Values may be sent and summed in bfloat16 or wider, within the bound.
A program may use at most 128 MiB of HBM per device.

v0:
```python
import math

import jax
import jax.numpy as jnp
from jax import lax
from jax.sharding import PartitionSpec as P

NLON = 10240
LB = 128
BLOCK = 128
BAS_DEV = 128


def per_device(spectra, legendre, wave_numbers, block_index, block_weights, basin_index):
    nwave = lax.axis_size("wave")
    ngroup = lax.axis_size("basin")
    fields, unused_parts, mloc, ncoef = spectra.shape
    lats = legendre.shape[2]
    latloc, nnz = block_index.shape
    nlon = NLON
    lon_block = LB
    blocks = nlon // lon_block
    nblk = 2 * nlon // BLOCK
    wavenum = lax.all_gather(wave_numbers, "wave", axis=0, tiled=True)
    sign = jnp.where(jnp.arange(ncoef) % 2 == 0, 1.0, -1.0).astype(jnp.bfloat16)
    both = jnp.stack([spectra, spectra * sign], axis=0)
    halves = jnp.einsum("hfrmj,mjl->hflrm", both, legendre, preferred_element_type=jnp.float32)
    north = halves[0]
    south = halves[1]
    sums_out = jnp.stack([north, south], axis=1).astype(jnp.bfloat16)
    sums_out = sums_out.reshape(fields * 2, lats * 2 * mloc)
    received = lax.all_to_all(sums_out, "wave", split_axis=1, concat_axis=1, tiled=True)
    received = received.reshape(fields, 2, nwave, latloc, 2, mloc)
    received = jnp.transpose(received, (0, 1, 3, 4, 2, 5))
    ncols = nwave * mloc
    rows = received.reshape(fields * 2 * latloc, 2, ncols).astype(jnp.float32)
    g_re = rows[:, 0, :]
    g_im = rows[:, 1, :]
    starts = jnp.arange(blocks, dtype=jnp.int32) * lon_block
    theta = (wavenum[None, :] * starts[:, None] % nlon).astype(jnp.float32) * (2.0 * math.pi / nlon)
    cos_a = jnp.cos(theta)
    sin_a = jnp.sin(theta)
    weight = jnp.where(wavenum == 0, 1.0, 2.0).astype(jnp.float32)
    offsets = jnp.arange(lon_block, dtype=jnp.int32)
    phi = (wavenum[:, None] * offsets[None, :] % nlon).astype(jnp.float32) * (2.0 * math.pi / nlon)
    basis = jnp.concatenate([jnp.cos(phi), -jnp.sin(phi)], axis=0).astype(jnp.bfloat16)
    scale = 1.0 / math.sqrt(2.0 * ncols)
    turned_re = (weight * (g_re[None] * cos_a[:, None] - g_im[None] * sin_a[:, None])).astype(
        jnp.bfloat16
    )
    turned_im = (weight * (g_re[None] * sin_a[:, None] + g_im[None] * cos_a[:, None])).astype(
        jnp.bfloat16
    )
    nrows = fields * 2 * latloc
    turned = jnp.concatenate([turned_re, turned_im], axis=2).reshape(blocks * nrows, 2 * ncols)
    lines = jnp.dot(turned, basis, preferred_element_type=jnp.float32) * scale
    lines = lines.reshape(blocks, nrows, lon_block).transpose(1, 0, 2).reshape(nrows, nlon)
    grid_fields = lines.astype(jnp.bfloat16).reshape(fields, 2, latloc, nlon)
    row_blocks = jnp.moveaxis(grid_fields, 1, 2).reshape(fields, latloc * nblk, BLOCK)
    local_index = block_index + jnp.arange(latloc, dtype=jnp.int32)[:, None] * nblk
    picked = jnp.take(row_blocks, local_index.reshape(-1), axis=1)
    row_values = jnp.einsum(
        "fep,ep->fe",
        picked,
        block_weights.reshape(latloc * nnz, BLOCK),
        preferred_element_type=jnp.float32,
    )
    basins = basin_index.reshape(-1)
    per_wave = BAS_DEV * ngroup
    dense = jnp.zeros((fields, per_wave * nwave), jnp.float32).at[:, basins].add(row_values)
    summed = lax.psum_scatter(dense, "wave", scatter_dimension=1, tiled=True)
    basin_sums = lax.all_to_all(summed, "basin", split_axis=1, concat_axis=0, tiled=True)
    return (grid_fields, basin_sums)


def solution(mesh):
    in_specs = (
        P("basin", None, "wave", None),
        P("wave", None, None),
        P("wave"),
        P("wave", None),
        P("wave", None, None),
        P("wave", None),
    )
    out_specs = (P("basin", None, "wave", None), P(None, ("wave", "basin")))
    return jax.shard_map(
        per_device, mesh=mesh, in_specs=in_specs, out_specs=out_specs, check_vma=False
    )
```

profile of v0, /device:TPU:1, one launch (start us, length us, event | category | flops | bytes accessed | tf_op | source)
XLA Modules:
  0.0 558.7 jit_solution(7812390682604152043)
XLA Ops:
  7.2 1.2 copy_bitcast_fusion
  8.4 0.8 copy-done
  9.2 0.8 fusion.22
  10.1 0.9 copy.37
  11.0 20.4 %all-to-all-start = ((bf16[8,128,20]{2,0,1:T(8,128)(2,1)}), bf16[8,128,20]{2,0,1:T(8,128)(2,1)S(1)}, u32[]{:S(2)}, u32[]{:S(2)}) async-start(bf16[8,128,20]{2,0,1:T(8,128)(2,1)} %copy.37), calls=%async_computation | async-start | bytes 524288 | tf_op jit(solution)/shard_map/all_to_all | solution.py:32
  31.4 0.0 reduce-scatter.2.cloned.1.call-start
  31.4 0.5 iota_multiply_fusion
  32.0 1.3 dynamic-slice
  33.9 0.3 dynamic-update-slice
  34.2 29.7 %all-reduce = s32[1280]{0:T(1024)S(1)} all-reduce(s32[1280]{0:T(1024)S(1)} %dynamic-update-slice), channel_id=1, replica_groups=mesh['wave'=128,'basin'=4] {'wave'}, use_global_device_ids=true, to_apply=%add | all-reduce | flops 1280 | bytes 10240
  63.9 3.9 cosine_convert_fusion
  67.8 1.3 compare_select_fusion.1
  69.1 0.7 compare_select_fusion
  69.8 0.6 broadcast_clamp_fusion
  70.4 3.3 fusion.44
  73.6 0.7 compare_and_fusion
  74.3 0.8 copy.48
  75.2 2.2 copy.39
  77.4 1.7 reshape.205
  79.1 2.2 fusion.9
  81.4 1.0 fusion.16
  82.4 0.7 copy-done.1
  83.1 0.1 copy.41
  83.2 7.5 %gather_fusion = bf16[1024,4,128]{2,1,0:T(4,128)(2,1)} fusion(bf16[4,160,128]{2,0,1:T(4,128)(2,1)S(1)} %copy.41, s32[1024]{0:T(1024)S(1)} %copy-done.5), kind=kCustom, calls=%fused_computation | custom fusion | bytes 2101248 | tf_op jit(solution)/shard_map/jit(_take)/gather | solution.py:61
  90.7 5.4 fusion.25
  96.1 19.6 %scatter_custom_fusion = f32[4,65536]{0,1:T(8,128)} fusion(s32[1024]{0:T(1024)} %bitcast.78, f32[1024,4]{1,0:T(8,128)} %bitcast.79, f32[]{:T(128)} %constant.62.clone.1), kind=kCustom, calls=%fused_computation.2 | custom fusion | flops 4096 | bytes 1049088 | tf_op jit(solution)/shard_map/scatter-add | solution.py:70
  115.7 425.8 %reduce-scatter.2.cloned.1.call-done = f32[4,512]{0,1:T(8,128)} async-done(((f32[4,65536]{0,1:T(8,128)}), f32[4,512]{0,1:T(8,128)}) %reduce-scatter.2.cloned.1.call-update) | async-done | bytes 8208 | tf_op jit(solution)/shard_map/reduce_scatter | solution.py:71
  541.5 1.7 copy.42
  543.2 3.9 all-to-all-start.1
  547.1 0.7 convert_element_type.85
  547.8 3.5 all-to-all-done.1
  551.3 0.6 copy.58
  (22 shorter events, 0.2 us)
Async XLA Ops:
  7.2 2.0 copy-start
  7.2 26.7 %copy-start.6 = (s32[10]{0:T(128)S(1)}, s32[10]{0:T(128)}, u32[]{:S(2)}) copy-start(s32[10]{0:T(128)} %param.8) | copy-start | bytes 124
  11.0 63.3 %all-to-all-start = ((bf16[8,128,20]{2,0,1:T(8,128)(2,1)}), bf16[8,128,20]{2,0,1:T(8,128)(2,1)S(1)}, u32[]{:S(2)}, u32[]{:S(2)}) async-start(bf16[8,128,20]{2,0,1:T(8,128)(2,1)} %copy.37), calls=%async_computation | async-start | bytes 524288 | tf_op jit(solution)/shard_map/all_to_all | solution.py:32
  31.4 510.2 %reduce-scatter.2.cloned.1.call-start = ((), (), s32[]{:S(2)}) async-start(), calls=%async_computation.3 | async-start | bytes 33816576 | tf_op jit(solution)/shard_map/reduce_scatter | solution.py:71
  79.1 2.3 copy-start.3
  79.1 2.3 copy-start.4
  81.4 1.8 copy-start.5
  82.4 0.7 copy-start.1
  115.7 431.4 %copy-start.2 = (bf16[80,8,128]{2,0,1:T(8,128)(2,1)S(1)}, bf16[80,8,128]{2,0,1:T(8,128)(2,1)}, u32[]{:S(2)}) copy-start(bf16[80,8,128]{2,0,1:T(8,128)(2,1)} %copy-done.1) | copy-start | bytes 491524
  543.2 8.1 %all-to-all-start.1 = ((f32[4,4,128]{2,0,1:T(4,128)}), f32[4,4,128]{2,0,1:T(4,128)S(1)}, u32[]{:S(2)}, u32[]{:S(2)}) async-start(f32[4,4,128]{2,0,1:T(4,128)} %copy.42), calls=%async_computation.2 | async-start | bytes 16384 | tf_op jit(solution)/shard_map/all_to_all | solution.py:72
Sparse Core Ops, SparseCore 0:
  115.8 425.6 reduce-scatter.1
where the time goes:
time: 569 us; the launch traced here: 559 us
  waiting for transfers between devices  429 us (75%)
  other arithmetic  34 us (6%)
  blocking collectives  29.7 us (5%)
  starting transfers between devices  24.4 us (4%)
  local copies, waits for them, and re-layouts  19.3 us (3%)
  between operations  14.9 us (3%)
  matrix products  7.2 us (1%)
    reduce_scatter x1, waiting for transfers between devices, per_device(): summed = lax.psum_scatter(dense, 'wave', scatter_dimension=1, tiled=True)  426 us
    unnamed x1, blocking collectives  29.7 us
    all_to_all x1, starting transfers between devices, per_device(): lax.all_to_all(sums_out, 'wave', split_axis=1, concat_axis=1, tiled=True)  20.4 us
    scatter-add x1, other arithmetic, per_device(): jnp.zeros((fields, per_wave * nwave), jnp.float32).at[:, basins]  19.6 us
  transfers between devices with their start and end apart: 3, of which 2 were waited for; matrix products, arithmetic and copies ran while one was open for 2% of the time, Pallas kernels for 0%

commit v1 on v0

v1 whole, which is shorter than its diff:
```python
import functools
import math

import jax
import jax.numpy as jnp
from jax import lax
from jax.experimental import pallas as pl
from jax.experimental.pallas import tpu as pltpu
from jax.sharding import PartitionSpec as P

NLON = 10240
LB = 128
BLOCK = 128
SLOTS = 16
BPW_BITS = 9
BPW = 1 << BPW_BITS
MESH = pl.DeviceIdType.MESH
F32 = jnp.float32
BF16 = jnp.bfloat16

COS_C = [(-1) ** n * math.pi ** (2 * n) / math.factorial(2 * n) for n in range(7)]
SIN_C = [(-1) ** n * math.pi ** (2 * n + 1) / math.factorial(2 * n + 1) for n in range(6)]


def cos_sin(r, turn):
    r = r - turn * jnp.floor(r * (1.0 / turn) + 0.5)
    y = r * (1.0 / turn)
    yy = y * y
    c = jnp.full_like(yy, COS_C[6])
    for k in range(5, -1, -1):
        c = c * yy + COS_C[k]
    s = jnp.full_like(yy, SIN_C[5])
    for k in range(4, -1, -1):
        s = s * yy + SIN_C[k]
    s = s * y
    return 1.0 - 2.0 * (s * s), 2.0 * (s * c)


def partner(k, me, nw):
    if nw != 128:
        return lax.rem(me + 1 + k, nw)
    x, z, c = me // 32, (me // 2) % 16, me % 2
    i, r = k // 8, k % 8
    zd = jnp.where(i % 2 == 0, 8 - i // 2, 8 + (i + 1) // 2)
    rx = r // 2
    xd = jnp.where(rx == 0, 2, jnp.where(rx == 1, 1, jnp.where(rx == 2, 3, 0)))
    cd = 1 - r % 2
    return (lax.rem(x + xd, 4) * 16 + lax.rem(z + zd, 16)) * 2 + lax.rem(c + cd, 2)


def iota(shape, dim):
    return lax.broadcasted_iota(jnp.int32, shape, dim)


def kernel(nw, ng, spec_ref, leg_hbm, wn_ref, blk_ref, wgt_ref, bas_ref,
           grid_hbm, sums_ref,
           leg, sa, ra, sb, rb, sd, rd, tu, ba, ws, one, vs, gr, pm,
           leg_sem, grid_sem, sa_sem, ra_sem, sb_sem, rb_sem, sd_sem, rd_sem):
    me, y = lax.axis_index("wave"), lax.axis_index("basin")
    mloc = leg.shape[0]
    nb, eb = bas_ref.shape
    nq = SLOTS * nw

    barrier = pltpu.get_barrier_semaphore()

    def greet(k, carry):
        pl.semaphore_signal(barrier, inc=1, device_id=(partner(k, me, nw), y), device_id_type=MESH)
        return carry

    lax.fori_loop(0, nw - 1, greet, 0)
    for k in range(1, ng):
        pl.semaphore_signal(barrier, inc=1, device_id=(me, lax.rem(y + k, ng)), device_id_type=MESH)

    for m in range(mloc):
        pltpu.make_async_copy(leg_hbm.at[m], leg.at[m], leg_sem.at[m]).start()

    bas = bas_ref[...]
    owner = bas >> BPW_BITS
    local = bas & (BPW - 1)
    upper = (iota((eb, eb), 0) < iota((eb, eb), 1)).astype(F32).astype(BF16)
    owned = [(owner[i:i + 1] == iota((nw, eb), 0)).astype(F32) for i in range(nb)]
    before = jnp.zeros((nw, 1), F32)
    ranks = []
    for i in range(nb):
        inside = jnp.dot(owned[i].astype(BF16), upper, preferred_element_type=F32)
        ranks.append(jnp.sum(owned[i] * (inside + before), axis=0, keepdims=True))
        before = before + jnp.sum(owned[i], axis=1, keepdims=True)
    lane = iota((128, eb), 0)
    where_to = jnp.zeros((nw, 128), F32)
    for i in range(nb):
        high = (local[i:i + 1] >> 7).astype(F32)
        low = (local[i:i + 1] & 127).astype(F32)
        rank = ranks[i].astype(jnp.int32)
        named = jnp.where(lane == rank + 96, high, 0.0) + jnp.where(lane == rank + 112, low, 0.0)
        where_to = where_to + lax.dot_general(
            owned[i].astype(BF16), named.astype(BF16), (((1,), (1,)), ((), ())),
            preferred_element_type=F32)
    rank_rows = jnp.concatenate(ranks, axis=0)
    place = rank_rows * float(nw) + owner.astype(F32)
    place_cols = jnp.transpose(place)

    ncoef = spec_ref.shape[3]
    odd = lax.rem(iota((8, ncoef), 1), 2) == 1
    sums = []
    for m in range(mloc):
        rows = jnp.concatenate([spec_ref[f, m].astype(F32) for f in range(4)], axis=0)
        both = jnp.concatenate([rows, jnp.where(odd, -rows, rows)], axis=0).astype(BF16)
        pltpu.make_async_copy(leg_hbm.at[m], leg.at[m], leg_sem.at[m]).wait()
        sums.append(jnp.dot(both, leg[m], preferred_element_type=F32))
    sums = jnp.concatenate(sums, axis=0)
    if mloc * 16 % 128:
        sums = jnp.concatenate([sums, jnp.zeros((256 - mloc * 16, nw), F32)], axis=0)
    by_lat = jnp.transpose(sums).astype(BF16)
    src = iota((256, 256), 0)
    dst = iota((256, 256), 1)
    r_of, lane_of = dst >> 7, dst & 127
    m_of, f_of, h_of = lane_of >> 3, (lane_of >> 1) & 3, lane_of & 1
    pick = (src == m_of * 16 + h_of * 8 + f_of * 2 + r_of) & (lane_of < mloc * 8)
    ordered = jnp.dot(by_lat, pick.astype(F32).astype(BF16), preferred_element_type=F32)
    lane = iota((1, 128), 1)
    numbers = jnp.zeros((1, 128), F32)
    for m in range(mloc):
        wn = wn_ref[m]
        numbers = numbers + jnp.where(lane == 80 + m, (wn >> 7).astype(F32), 0.0)
        numbers = numbers + jnp.where(lane == 96 + m, (wn & 127).astype(F32), 0.0)
    part_re = ordered[:, :128] + numbers
    part_im = ordered[:, 128:] + where_to
    sa[...] = jnp.concatenate([part_re[:, None, :], part_im[:, None, :]], axis=1).astype(BF16)

    pl.semaphore_wait(barrier, nw - 1 + ng - 1)

    def send_a(k, carry):
        to = partner(k, me, nw)
        pltpu.make_async_remote_copy(
            src_ref=sa.at[pl.ds(to, 1)], dst_ref=ra.at[pl.ds(me, 1)], send_sem=sa_sem,
            recv_sem=ra_sem, device_id=(to, y), device_id_type=MESH).start()
        return carry

    lax.fori_loop(0, nw - 1, send_a, 0)
    ra[pl.ds(me, 1)] = sa[pl.ds(me, 1)]

    ext = jnp.concatenate(
        [jnp.concatenate([blk_ref[i:i + 1].astype(F32), jnp.zeros((15, eb), F32)], axis=0)
         for i in range(nb)], axis=1)
    turned_w = jnp.concatenate(
        [jnp.transpose(wgt_ref[i * eb:(i + 1) * eb].astype(F32)) for i in range(nb)], axis=1)
    left = jnp.concatenate([turned_w, ext], axis=0).astype(BF16)
    for i in range(nb):
        col = jnp.broadcast_to(place_cols[:, i:i + 1], (eb, 128 if nq >= 128 else nq))
        for c in range(max(1, nq // 128)):
            spot = (iota(col.shape, 1) + c * 128).astype(F32)
            pm[i * eb:(i + 1) * eb, c * 128:c * 128 + col.shape[1]] = jnp.where(
                col == spot, 1.0, 0.0).astype(BF16)
    qc = min(256, nq)
    for c in range(nq // qc):
        ws[:, c * qc:(c + 1) * qc] = jnp.dot(
            left, pm[:, c * qc:(c + 1) * qc], preferred_element_type=F32).astype(BF16)
    vs[...] = jnp.zeros(vs.shape, F32)

    pltpu.make_async_copy(sa.at[pl.ds(0, nw - 1)], ra.at[pl.ds(0, nw - 1)], ra_sem).wait()

    got = ra[...].astype(F32)
    re, im = got[:, 0, :], got[:, 1, :]
    re_t, im_t = jnp.transpose(re), jnp.transpose(im)
    m_rows = re_t[80:96] * 128.0 + re_t[96:112]
    a_of = (iota((80, nw), 0) >> 1).astype(F32)
    parity = lax.rem(iota((8, nw), 0), 2) == 0
    ncols = mloc * nw
    b_of = iota((nw, LB), 1).astype(F32)
    for m in range(mloc):
        number = m_rows[m:m + 1]
        weight = jnp.where(number == 0.0, 1.0, 2.0)
        cos_a, sin_a = cos_sin(number * a_of, 80.0)
        cos_a, sin_a = cos_a.reshape(10, 8, nw), sin_a.reshape(10, 8, nw)
        g_re = re_t[m * 8:(m + 1) * 8] * weight
        g_im = im_t[m * 8:(m + 1) * 8] * weight
        for f in range(4):
            fr = jnp.where(parity, g_re[2 * f:2 * f + 1], g_re[2 * f + 1:2 * f + 2])[None]
            fi = jnp.where(parity, g_im[2 * f:2 * f + 1], g_im[2 * f + 1:2 * f + 2])[None]
            t_re = (fr * cos_a - fi * sin_a).reshape(80, nw)
            t_im = (fr * sin_a + fi * cos_a).reshape(80, nw)
            tu[f * 80:(f + 1) * 80, m * nw:(m + 1) * nw] = t_re.astype(BF16)
            tu[f * 80:(f + 1) * 80, ncols + m * nw:ncols + (m + 1) * nw] = t_im.astype(BF16)
        column = re[:, 80 + m:81 + m] * 128.0 + re[:, 96 + m:97 + m]
        cos_b, sin_b = cos_sin(column * b_of, float(NLON))
        flip = 1.0 - 2.0 * (column - 2.0 * jnp.floor(column * 0.5))
        rows = slice(m * nw, (m + 1) * nw)
        ba[rows, :128] = cos_b.astype(BF16)
        ba[rows, 128:] = (cos_b * flip).astype(BF16)
        rows = slice(ncols + m * nw, ncols + (m + 1) * nw)
        ba[rows, :128] = (-sin_b).astype(BF16)
        ba[rows, 128:] = (-sin_b * flip).astype(BF16)
    scale = 1.0 / math.sqrt(2.0 * ncols)
    for f in range(4):
        lines = jnp.dot(tu[f * 80:(f + 1) * 80], ba[...], preferred_element_type=F32) * scale
        gr[f, :80] = lines[:, :128].astype(BF16)
        gr[f, 80:] = lines[:, 128:].astype(BF16)

    row = iota((160, qc), 0)
    block_of = (row & 1) * 80 + (row >> 1)
    block_of = block_of.astype(F32)
    for c in range(nq // qc):
        cols = slice(c * qc, (c + 1) * qc)
        hit = block_of == ws[128:129, cols].astype(F32)
        for f in range(4):
            prod = jnp.dot(gr[f], ws[:128, cols], preferred_element_type=F32)
            val = jnp.sum(jnp.where(hit, prod, 0.0), axis=0, keepdims=True)
            for j in range(qc // nw):
                s = c * (qc // nw) + j
                vs[s * 4 + f:s * 4 + f + 1, :nw] = val[:, j * nw:(j + 1) * nw]
    sb[...] = jnp.transpose(vs[...])

    def send_b(k, carry):
        to = partner(k, me, nw)
        pltpu.make_async_remote_copy(
            src_ref=sb.at[pl.ds(to, 1)], dst_ref=rb.at[pl.ds(me, 1)], send_sem=sb_sem,
            recv_sem=rb_sem, device_id=(to, y), device_id_type=MESH).start()
        return carry

    lax.fori_loop(0, nw - 1, send_b, 0)
    rb[pl.ds(me, 1)] = sb[pl.ds(me, 1)]
    out = pltpu.make_async_copy(gr, grid_hbm, grid_sem)
    out.start()

    basin = iota((nw, BPW), 1).astype(F32)
    for s in range(SLOTS):
        column = im[:, 96 + s:97 + s] * 128.0 + im[:, 112 + s:113 + s]
        one[s * nw:(s + 1) * nw] = jnp.where(column == basin, 1.0, 0.0).astype(BF16)

    pltpu.make_async_copy(sb.at[pl.ds(0, nw - 1)], rb.at[pl.ds(0, nw - 1)], rb_sem).wait()
    val = jnp.transpose(rb[...])
    val = jnp.concatenate([val[s * 4:(s + 1) * 4] for s in range(SLOTS)], axis=1)
    high = val.astype(BF16).astype(F32)
    pair = jnp.concatenate([high, val - high], axis=0).astype(BF16)
    dense = jnp.dot(pair, one[...], preferred_element_type=F32)
    dense = dense[:4] + dense[4:]
    width = BPW // ng
    for g in range(ng):
        sd[g] = dense[:, g * width:(g + 1) * width]
    moves = []
    for k in range(1, ng):
        to = lax.rem(y + k, ng)
        moves.append(pltpu.make_async_remote_copy(
            src_ref=sd.at[to], dst_ref=rd.at[y], send_sem=sd_sem, recv_sem=rd_sem,
            device_id=(me, to), device_id_type=MESH))
        moves[-1].start()
    rd[y] = sd[y]
    pltpu.make_async_copy(sd.at[pl.ds(0, ng - 1)], rd.at[pl.ds(0, ng - 1)], rd_sem).wait()
    sums_ref[...] = rd[...]

    out.wait()
    pltpu.make_async_copy(sa.at[pl.ds(0, nw - 1)], ra.at[pl.ds(0, nw - 1)], sa_sem).wait()
    pltpu.make_async_copy(sb.at[pl.ds(0, nw - 1)], rb.at[pl.ds(0, nw - 1)], sb_sem).wait()
    pltpu.make_async_copy(sd.at[pl.ds(0, ng - 1)], rd.at[pl.ds(0, ng - 1)], sd_sem).wait()


def per_device(spectra, legendre, wave_numbers, block_index, block_weights, basin_index):
    nw, ng = lax.axis_size("wave"), lax.axis_size("basin")
    mloc, ncoef, lats = legendre.shape
    nnz = block_index.shape[1]
    eb = min(128, nnz)
    nq = SLOTS * nw
    width = BPW // ng
    vmem = pl.BlockSpec(memory_space=pltpu.VMEM)
    grid, sums = pl.pallas_call(
        functools.partial(kernel, nw, ng),
        out_shape=(jax.ShapeDtypeStruct((4, 160, 128), BF16),
                   jax.ShapeDtypeStruct((ng, 4, width), F32)),
        in_specs=[vmem, pl.BlockSpec(memory_space=pl.ANY), pl.BlockSpec(memory_space=pltpu.SMEM),
                  vmem, vmem, vmem],
        out_specs=(pl.BlockSpec(memory_space=pl.ANY), vmem),
        scratch_shapes=[
            pltpu.VMEM((mloc, ncoef, lats), BF16),
            pltpu.VMEM((nw, 2, 128), BF16),
            pltpu.VMEM((nw, 2, 128), BF16),
            pltpu.VMEM((nw, 128), F32),
            pltpu.VMEM((nw, 128), F32),
            pltpu.VMEM((ng, 4, width), F32),
            pltpu.VMEM((ng, 4, width), F32),
            pltpu.VMEM((320, 2 * mloc * nw), BF16),
            pltpu.VMEM((2 * mloc * nw, 256), BF16),
            pltpu.VMEM((144, nq), BF16),
            pltpu.VMEM((nq, BPW), BF16),
            pltpu.VMEM((128, nw), F32),
            pltpu.VMEM((4, 160, 128), BF16),
            pltpu.VMEM((nnz, nq), BF16),
            pltpu.SemaphoreType.DMA((mloc,)),
            pltpu.SemaphoreType.DMA,
            pltpu.SemaphoreType.DMA,
            pltpu.SemaphoreType.DMA,
            pltpu.SemaphoreType.DMA,
            pltpu.SemaphoreType.DMA,
            pltpu.SemaphoreType.DMA,
            pltpu.SemaphoreType.DMA,
        ],
        compiler_params=pltpu.CompilerParams(
            collective_id=0, has_side_effects=True, vmem_limit_bytes=40 * 1024 * 1024),
    )(jnp.transpose(spectra, (0, 2, 1, 3)), legendre, wave_numbers,
      block_index.reshape(nnz // eb, eb), block_weights.reshape(nnz, BLOCK),
      basin_index.reshape(nnz // eb, eb))
    grid = jnp.transpose(grid.reshape(4, 80, 2, 128), (0, 2, 1, 3)).reshape(4, 2, 1, NLON)
    return grid, sums.reshape(ng * 4, width)


def solution(mesh):
    in_specs = (
        P("basin", None, "wave", None),
        P("wave", None, None),
        P("wave"),
        P("wave", None),
        P("wave", None, None),
        P("wave", None),
    )
    out_specs = (P("basin", None, "wave", None), P(None, ("wave", "basin")))
    return jax.shard_map(
        per_device, mesh=mesh, in_specs=in_specs, out_specs=out_specs, check_vma=False
    )
```

time: 569 us -> 57.6 us (0.10); the launches traced: 559 us -> 57.3 us
  waiting for transfers between devices: 429 us -> 0 us
  Pallas kernels: 0 us -> 49.5 us
  other arithmetic: 34 us -> 0 us
  blocking collectives: 29.7 us -> 0 us
  starting transfers between devices: 24.4 us -> 0 us
  between operations: 14.9 us -> 0.65 us
  local copies, waits for them, and re-layouts: 19.3 us -> 7.09 us
  matrix products: 7.2 us -> 0 us
    reduce_scatter x1 -> x0, waiting for transfers between devices: 426 us -> none  [per_device(): summed = lax.psum_scatter(dense, 'wave', scatter_dimension=1, tiled=True)]
    pallas_call x0 -> x1, Pallas kernels: none -> 49.5 us  [per_device(): pl.pallas_call(functools.partial(kernel, nw, ng), out_shape=(jax.ShapeDty...]
    unnamed x1 -> x0, blocking collectives: 29.7 us -> none
    all_to_all x2 -> x0, starting transfers between devices: 24.3 us -> none  [the longest x1 20.4 us: per_device(): lax.all_to_all(sums_out, 'wave', split_axis=1, concat_axis=1, tiled=True)]
    scatter-add x1 -> x0, other arithmetic: 19.6 us -> none  [per_device(): jnp.zeros((fields, per_wave * nwave), jnp.float32).at[:, basins]]
    gather x1 -> x0, local copies, waits for them, and re-layouts: 7.5 us -> none  [per_device(): picked = jnp.take(row_blocks, local_index.reshape(-1), axis=1)]
    dot_general x3 -> x0, matrix products: 7.2 us -> none  [the longest x1 5.42 us: per_device(): jnp.einsum('fep,ep->fe', picked, block_weights.reshape(latloc * nnz, BLOC...]
  transfers between devices with their start and end apart: 3 -> 0, of which waited for: 2 -> 0; matrix products, arithmetic and copies ran while one was open for 2% -> 0% of each run, Pallas kernels for 0% -> 0%
where the time goes in v1:
time: 57.6 us; the launch traced here: 57.3 us
  Pallas kernels  49.5 us (86%)
  local copies, waits for them, and re-layouts  7.09 us (12%)
  between operations  0.65 us (1%)
    pallas_call x1, Pallas kernels, per_device(): pl.pallas_call(functools.partial(kernel, nw, ng), out_shape=(jax.ShapeDty...  49.5 us
    unnamed x14, local copies, waits for them, and re-layouts  7.09 us

profile of v1, /device:TPU:1, one launch (start us, length us, event | category | flops | bytes accessed | tf_op | source)
XLA Modules:
  0.0 57.3 jit_solution(9147848590394005292)
XLA Ops:
  0.6 0.0 copy-start
  0.6 1.9 %copy-done = bf16[10,1280,128]{2,1,0:T(8,128)(2,1)S(1)} copy-done((bf16[10,1280,128]{2,1,0:T(8,128)(2,1)S(1)}, bf16[10,1280,128]{2,1,0:T(8,128)(2,1)}, u32[]{:S(2)}) %copy-start) | copy-done | bytes 3276824
  2.6 0.0 copy-start.1
  2.6 0.9 %copy-done.1 = bf16[1,1024,128]{2,1,0:T(8,128)(2,1)S(1)} copy-done((bf16[1,1024,128]{2,1,0:T(8,128)(2,1)S(1)}, bf16[1,1024,128]{2,1,0:T(8,128)(2,1)}, u32[]{:S(2)}) %copy-start.1) | copy-done | bytes 262168
  3.5 0.0 copy-start.2
  3.5 0.9 %copy-done.2 = bf16[4,2,10,1280]{3,1,2,0:T(2,128)(2,1)S(1)} copy-done((bf16[4,2,10,1280]{3,1,2,0:T(2,128)(2,1)S(1)}, bf16[4,2,10,1280]{3,1,2,0:T(2,128)(2,1)}, u32[]{:S(2)}) %copy-start.2) | copy-done | bytes 204824
  4.4 0.0 copy-start.3
  4.4 0.7 %copy-done.3 = s32[1,1024]{1,0:T(1,128)S(1)} copy-done((s32[1,1024]{1,0:T(1,128)S(1)}, s32[1,1024]{1,0:T(1,128)}, u32[]{:S(2)}) %copy-start.3) | copy-done | bytes 4120
  5.1 0.0 copy-start.4
  5.1 0.7 %copy-done.4 = s32[1,1024]{1,0:T(1,128)S(1)} copy-done((s32[1,1024]{1,0:T(1,128)S(1)}, s32[1,1024]{1,0:T(1,128)}, u32[]{:S(2)}) %copy-start.4) | copy-done | bytes 4120
  5.8 0.0 copy-start.5
  5.8 0.7 %copy-done.5 = s32[10]{0:T(128)S(1)} copy-done((s32[10]{0:T(128)S(1)}, s32[10]{0:T(128)}, u32[]{:S(2)}) %copy-start.5) | copy-done | bytes 64
  6.5 49.5 %shard_map.77 = (bf16[4,160,128]{2,1,0:T(8,128)(2,1)S(1)}, f32[4,4,128]{2,1,0:T(4,128)S(1)}) custom-call(bf16[4,10,2,1280]{3,2,1,0:T(2,128)(2,1)S(1)} %bitcast.11, bf16[10,1280,128]{2,1,0:T(8,128)(2,1)S(1)} %copy-done, s32[10]{0:T(128)S(1)} %copy-done.5, s32[8,128]{1,0:T(8,128)S(1)} %bitcast.14, bf16[1024,128]{1,0:T(8,128)(2,1)S(1)} %bitcast.10, ...), custom_call_target="tpu_custom_call" | custom-call | tf_op jit(solution)/shard_map/pallas_call | solution.py:265
  56.0 0.7 %copy.11 = bf16[4,2,1,10240]{3,1,2,0:T(2,128)(2,1)} copy(bf16[4,2,1,10240]{3,1,2,0:T(2,128)(2,1)S(1)} %bitcast.12) | data formatting | bytes 327680
  56.7 0.6 %copy.12 = f32[16,128]{1,0:T(8,128)} copy(f32[16,128]{1,0:T(8,128)S(1)} %bitcast.13) | data formatting | bytes 16384
Async XLA Ops:
  0.6 1.9 %copy-start = (bf16[10,1280,128]{2,1,0:T(8,128)(2,1)S(1)}, bf16[10,1280,128]{2,1,0:T(8,128)(2,1)}, u32[]{:S(2)}) copy-start(bf16[10,1280,128]{2,1,0:T(8,128)(2,1)} %leg_hbm.1) | copy-start | bytes 9830404
  2.6 0.9 %copy-start.1 = (bf16[1,1024,128]{2,1,0:T(8,128)(2,1)S(1)}, bf16[1,1024,128]{2,1,0:T(8,128)(2,1)}, u32[]{:S(2)}) copy-start(bf16[1,1024,128]{2,1,0:T(8,128)(2,1)} %param.10) | copy-start | bytes 786436
  3.5 0.9 %copy-start.2 = (bf16[4,2,10,1280]{3,1,2,0:T(2,128)(2,1)S(1)}, bf16[4,2,10,1280]{3,1,2,0:T(2,128)(2,1)}, u32[]{:S(2)}) copy-start(bf16[4,2,10,1280]{3,1,2,0:T(2,128)(2,1)} %param.6) | copy-start | bytes 614404
  4.4 0.7 %copy-start.3 = (s32[1,1024]{1,0:T(1,128)S(1)}, s32[1,1024]{1,0:T(1,128)}, u32[]{:S(2)}) copy-start(s32[1,1024]{1,0:T(1,128)} %param.9) | copy-start | bytes 12292
  5.1 0.7 %copy-start.4 = (s32[1,1024]{1,0:T(1,128)S(1)}, s32[1,1024]{1,0:T(1,128)}, u32[]{:S(2)}) copy-start(s32[1,1024]{1,0:T(1,128)} %param.11) | copy-start | bytes 12292
  5.8 0.7 %copy-start.5 = (s32[10]{0:T(128)S(1)}, s32[10]{0:T(128)}, u32[]{:S(2)}) copy-start(s32[10]{0:T(128)} %wn_ref.1) | copy-start | bytes 124

commit v2 on v1

--- a/solution.py
+++ b/solution.py
@@ -36,26 +36,32 @@
     return 1.0 - 2.0 * (s * s), 2.0 * (s * c)
 
 
-def partner(k, me, nw):
+def each_other(me, nw, act):
     if nw != 128:
-        return lax.rem(me + 1 + k, nw)
-    x, z, c = me // 32, (me // 2) % 16, me % 2
-    i, r = k // 8, k % 8
-    zd = jnp.where(i % 2 == 0, 8 - i // 2, 8 + (i + 1) // 2)
-    rx = r // 2
-    xd = jnp.where(rx == 0, 2, jnp.where(rx == 1, 1, jnp.where(rx == 2, 3, 0)))
-    cd = 1 - r % 2
-    return (lax.rem(x + xd, 4) * 16 + lax.rem(z + zd, 16)) * 2 + lax.rem(c + cd, 2)
+        lax.fori_loop(1, nw, lambda k, carry: (act(lax.rem(me + k, nw)), carry)[1], 0)
+        return
+    x, z, c = me >> 5, (me >> 1) & 15, me & 1
+    planes = [(((x + xd) & 3) << 5) | (c ^ cd) for xd in (2, 1, 3, 0) for cd in (1, 0)]
+
+    def level(i, carry):
+        there = ((z + 8 + ((i + 1) >> 1) * (2 * (i & 1) - 1)) & 15) << 1
+        for plane in planes:
+            act(plane | there)
+        return carry
+
+    lax.fori_loop(0, 15, level, 0)
+    for plane in planes[:-1]:
+        act(plane | (z << 1))
 
 
 def iota(shape, dim):
     return lax.broadcasted_iota(jnp.int32, shape, dim)
 
 
-def kernel(nw, ng, spec_ref, leg_hbm, wn_ref, blk_ref, wgt_ref, bas_ref,
+def kernel(nw, ng, spec_hbm, leg_hbm, wn_hbm, blk_hbm, wgt_hbm, bas_hbm,
            grid_hbm, sums_ref,
-           leg, sa, ra, sb, rb, sd, rd, tu, ba, ws, one, vs, gr, pm,
-           leg_sem, grid_sem, sa_sem, ra_sem, sb_sem, rb_sem, sd_sem, rd_sem):
+           spec_ref, wn_ref, blk_ref, wgt_ref, bas_ref, leg, sa, ra, sb, rb, sd, rd, tu, ba, ca, sn, ws, one, vs, gr, pm,
+           in_sem, leg_sem, grid_sem, sa_sem, ra_sem, sb_sem, rb_sem, sd_sem, rd_sem):
     me, y = lax.axis_index("wave"), lax.axis_index("basin")
     mloc = leg.shape[0]
     nb, eb = bas_ref.shape
@@ -63,17 +69,24 @@
 
     barrier = pltpu.get_barrier_semaphore()
 
-    def greet(k, carry):
-        pl.semaphore_signal(barrier, inc=1, device_id=(partner(k, me, nw), y), device_id_type=MESH)
-        return carry
-
-    lax.fori_loop(0, nw - 1, greet, 0)
+    def greet(to):
+        pl.semaphore_signal(barrier, inc=1, device_id=(to, y), device_id_type=MESH)
+
+    each_other(me, nw, greet)
     for k in range(1, ng):
         pl.semaphore_signal(barrier, inc=1, device_id=(me, lax.rem(y + k, ng)), device_id_type=MESH)
 
+    bring = [pltpu.make_async_copy(*pair, in_sem.at[i]) for i, pair in enumerate((
+        (bas_hbm, bas_ref), (spec_hbm, spec_ref), (wn_hbm, wn_ref), (blk_hbm, blk_ref),
+        (wgt_hbm, wgt_ref)))]
+    for copy in bring[:2]:
+        copy.start()
     for m in range(mloc):
         pltpu.make_async_copy(leg_hbm.at[m], leg.at[m], leg_sem.at[m]).start()
-
+    for copy in bring[2:]:
+        copy.start()
+
+    bring[0].wait()
     bas = bas_ref[...]
     owner = bas >> BPW_BITS
     local = bas & (BPW - 1)
@@ -101,6 +114,7 @@
 
     ncoef = spec_ref.shape[3]
     odd = lax.rem(iota((8, ncoef), 1), 2) == 1
+    bring[1].wait()
     sums = []
     for m in range(mloc):
         rows = jnp.concatenate([spec_ref[f, m].astype(F32) for f in range(4)], axis=0)
@@ -119,6 +133,7 @@
     ordered = jnp.dot(by_lat, pick.astype(F32).astype(BF16), preferred_element_type=F32)
     lane = iota((1, 128), 1)
     numbers = jnp.zeros((1, 128), F32)
+    bring[2].wait()
     for m in range(mloc):
         wn = wn_ref[m]
         numbers = numbers + jnp.where(lane == 80 + m, (wn >> 7).astype(F32), 0.0)
@@ -129,16 +144,16 @@
 
     pl.semaphore_wait(barrier, nw - 1 + ng - 1)
 
-    def send_a(k, carry):
-        to = partner(k, me, nw)
+    def send_a(to):
         pltpu.make_async_remote_copy(
             src_ref=sa.at[pl.ds(to, 1)], dst_ref=ra.at[pl.ds(me, 1)], send_sem=sa_sem,
             recv_sem=ra_sem, device_id=(to, y), device_id_type=MESH).start()
-        return carry
-
-    lax.fori_loop(0, nw - 1, send_a, 0)
+
+    each_other(me, nw, send_a)
     ra[pl.ds(me, 1)] = sa[pl.ds(me, 1)]
 
+    bring[3].wait()
+    bring[4].wait()
     ext = jnp.concatenate(
         [jnp.concatenate([blk_ref[i:i + 1].astype(F32), jnp.zeros((15, eb), F32)], axis=0)
          for i in range(nb)], axis=1)
@@ -155,46 +170,54 @@
     for c in range(nq // qc):
         ws[:, c * qc:(c + 1) * qc] = jnp.dot(
             left, pm[:, c * qc:(c + 1) * qc], preferred_element_type=F32).astype(BF16)
-    vs[...] = jnp.zeros(vs.shape, F32)
+
+    a_of = (iota((80, 128), 0) >> 1).astype(F32)
+    lane_of = iota((1, 128), 1).astype(F32)
+    m_of, b_of = iota((128, LB), 0).astype(F32), iota((128, LB), 1).astype(F32)
+    flip = 1.0 - 2.0 * (iota((128, LB), 0) & 1).astype(F32)
+    for hi in range(10):
+        number = lane_of + 128.0 * hi
+        weight = jnp.where(number == 0.0, 1.0, 2.0)
+        cos_a, sin_a = cos_sin(number * a_of, 80.0)
+        ca[hi], sn[hi] = cos_a * weight, sin_a * weight
+        cos_b, sin_b = cos_sin((m_of + 128.0 * hi) * b_of, float(NLON))
+        ba[hi * 256:hi * 256 + 128, :128] = cos_b.astype(BF16)
+        ba[hi * 256:hi * 256 + 128, 128:] = (cos_b * flip).astype(BF16)
+        ba[hi * 256 + 128:hi * 256 + 256, :128] = (-sin_b).astype(BF16)
+        ba[hi * 256 + 128:hi * 256 + 256, 128:] = (-sin_b * flip).astype(BF16)
 
     pltpu.make_async_copy(sa.at[pl.ds(0, nw - 1)], ra.at[pl.ds(0, nw - 1)], ra_sem).wait()
 
     got = ra[...].astype(F32)
     re, im = got[:, 0, :], got[:, 1, :]
     re_t, im_t = jnp.transpose(re), jnp.transpose(im)
-    m_rows = re_t[80:96] * 128.0 + re_t[96:112]
-    a_of = (iota((80, nw), 0) >> 1).astype(F32)
-    parity = lax.rem(iota((8, nw), 0), 2) == 0
-    ncols = mloc * nw
-    b_of = iota((nw, LB), 1).astype(F32)
+    low_lane = iota((nw, 128), 1).astype(F32)
+    lefts, rights = [], []
     for m in range(mloc):
-        number = m_rows[m:m + 1]
-        weight = jnp.where(number == 0.0, 1.0, 2.0)
-        cos_a, sin_a = cos_sin(number * a_of, 80.0)
-        cos_a, sin_a = cos_a.reshape(10, 8, nw), sin_a.reshape(10, 8, nw)
-        g_re = re_t[m * 8:(m + 1) * 8] * weight
-        g_im = im_t[m * 8:(m + 1) * 8] * weight
+        both = jnp.concatenate([re_t[m * 8:(m + 1) * 8], im_t[m * 8:(m + 1) * 8]], axis=0)
+        high = re_t[80 + m:81 + m]
+        lefts.append(jnp.concatenate(
+            [jnp.where(high == float(hi), both, 0.0) for hi in range(10)], axis=0).astype(BF16))
+        rights.append(jnp.where(re[:, 96 + m:97 + m] == low_lane, 1.0, 0.0).astype(BF16))
+    columns = jnp.dot(jnp.concatenate(lefts, axis=1), jnp.concatenate(rights, axis=0),
+                      preferred_element_type=F32)
+
+    parity = (iota((8, 128), 0) & 1) == 0
+    for hi in range(10):
+        cos_a, sin_a = ca[hi].reshape(10, 8, 128), sn[hi].reshape(10, 8, 128)
+        g_re, g_im = columns[hi * 16:hi * 16 + 8], columns[hi * 16 + 8:hi * 16 + 16]
         for f in range(4):
             fr = jnp.where(parity, g_re[2 * f:2 * f + 1], g_re[2 * f + 1:2 * f + 2])[None]
             fi = jnp.where(parity, g_im[2 * f:2 * f + 1], g_im[2 * f + 1:2 * f + 2])[None]
-            t_re = (fr * cos_a - fi * sin_a).reshape(80, nw)
-            t_im = (fr * sin_a + fi * cos_a).reshape(80, nw)
-            tu[f * 80:(f + 1) * 80, m * nw:(m + 1) * nw] = t_re.astype(BF16)
-            tu[f * 80:(f + 1) * 80, ncols + m * nw:ncols + (m + 1) * nw] = t_im.astype(BF16)
-        column = re[:, 80 + m:81 + m] * 128.0 + re[:, 96 + m:97 + m]
-        cos_b, sin_b = cos_sin(column * b_of, float(NLON))
-        flip = 1.0 - 2.0 * (column - 2.0 * jnp.floor(column * 0.5))
-        rows = slice(m * nw, (m + 1) * nw)
-        ba[rows, :128] = cos_b.astype(BF16)
-        ba[rows, 128:] = (cos_b * flip).astype(BF16)
-        rows = slice(ncols + m * nw, ncols + (m + 1) * nw)
-        ba[rows, :128] = (-sin_b).astype(BF16)
-        ba[rows, 128:] = (-sin_b * flip).astype(BF16)
-    scale = 1.0 / math.sqrt(2.0 * ncols)
+            t_re = (fr * cos_a - fi * sin_a).reshape(80, 128)
+            t_im = (fr * sin_a + fi * cos_a).reshape(80, 128)
+            tu[f * 80:(f + 1) * 80, hi * 256:hi * 256 + 128] = t_re.astype(BF16)
+            tu[f * 80:(f + 1) * 80, hi * 256 + 128:hi * 256 + 256] = t_im.astype(BF16)
+    scale = 1.0 / math.sqrt(2.0 * mloc * nw)
+    lines = jnp.dot(tu[...], ba[...], preferred_element_type=F32) * scale
     for f in range(4):
-        lines = jnp.dot(tu[f * 80:(f + 1) * 80], ba[...], preferred_element_type=F32) * scale
-        gr[f, :80] = lines[:, :128].astype(BF16)
-        gr[f, 80:] = lines[:, 128:].astype(BF16)
+        gr[f, :80] = lines[f * 80:(f + 1) * 80, :128].astype(BF16)
+        gr[f, 80:] = lines[f * 80:(f + 1) * 80, 128:].astype(BF16)
 
     row = iota((160, qc), 0)
     block_of = (row & 1) * 80 + (row >> 1)
@@ -202,41 +225,45 @@
     for c in range(nq // qc):
         cols = slice(c * qc, (c + 1) * qc)
         hit = block_of == ws[128:129, cols].astype(F32)
-        for f in range(4):
-            prod = jnp.dot(gr[f], ws[:128, cols], preferred_element_type=F32)
-            val = jnp.sum(jnp.where(hit, prod, 0.0), axis=0, keepdims=True)
-            for j in range(qc // nw):
-                s = c * (qc // nw) + j
-                vs[s * 4 + f:s * 4 + f + 1, :nw] = val[:, j * nw:(j + 1) * nw]
+        prod = jnp.dot(gr[...].reshape(640, 128), ws[:128, cols], preferred_element_type=F32)
+        val = jnp.concatenate(
+            [jnp.sum(jnp.where(hit, prod[f * 160:(f + 1) * 160], 0.0), axis=0, keepdims=True)
+             for f in range(4)], axis=0)
+        high = val.astype(BF16).astype(F32)
+        val = jnp.concatenate([high, val - high], axis=0)
+        for j in range(qc // nw):
+            s = c * (qc // nw) + j
+            vs[s * 8:(s + 1) * 8] = val[:, j * nw:(j + 1) * nw]
     sb[...] = jnp.transpose(vs[...])
 
-    def send_b(k, carry):
-        to = partner(k, me, nw)
+    def send_b(to):
         pltpu.make_async_remote_copy(
             src_ref=sb.at[pl.ds(to, 1)], dst_ref=rb.at[pl.ds(me, 1)], send_sem=sb_sem,
             recv_sem=rb_sem, device_id=(to, y), device_id_type=MESH).start()
-        return carry
-
-    lax.fori_loop(0, nw - 1, send_b, 0)
+
+    each_other(me, nw, send_b)
     rb[pl.ds(me, 1)] = sb[pl.ds(me, 1)]
     out = pltpu.make_async_copy(gr, grid_hbm, grid_sem)
     out.start()
 
-    basin = iota((nw, BPW), 1).astype(F32)
     for s in range(SLOTS):
-        column = im[:, 96 + s:97 + s] * 128.0 + im[:, 112 + s:113 + s]
-        one[s * nw:(s + 1) * nw] = jnp.where(column == basin, 1.0, 0.0).astype(BF16)
+        one[s * nw:(s + 1) * nw] = jnp.where(
+            im[:, 112 + s:113 + s] == low_lane, 1.0, 0.0).astype(BF16)
 
     pltpu.make_async_copy(sb.at[pl.ds(0, nw - 1)], rb.at[pl.ds(0, nw - 1)], rb_sem).wait()
     val = jnp.transpose(rb[...])
-    val = jnp.concatenate([val[s * 4:(s + 1) * 4] for s in range(SLOTS)], axis=1)
-    high = val.astype(BF16).astype(F32)
-    pair = jnp.concatenate([high, val - high], axis=0).astype(BF16)
-    dense = jnp.dot(pair, one[...], preferred_element_type=F32)
-    dense = dense[:4] + dense[4:]
-    width = BPW // ng
+    named = []
+    for s in range(SLOTS):
+        high = im_t[96 + s:97 + s]
+        named.append(jnp.concatenate(
+            [jnp.where(high == float(hi), val[s * 8:(s + 1) * 8], 0.0) for hi in range(BPW // 128)],
+            axis=0).astype(BF16))
+    dense = jnp.dot(jnp.concatenate(named, axis=1), one[...], preferred_element_type=F32)
+    dense = [dense[hi * 8:hi * 8 + 4] + dense[hi * 8 + 4:hi * 8 + 8] for hi in range(BPW // 128)]
+    each = BPW // 128 // ng
     for g in range(ng):
-        sd[g] = dense[:, g * width:(g + 1) * width]
+        for k in range(each):
+            sd[g, :, k * 128:(k + 1) * 128] = dense[g * each + k]
     moves = []
     for k in range(1, ng):
         to = lax.rem(y + k, ng)
@@ -266,10 +293,14 @@
         functools.partial(kernel, nw, ng),
         out_shape=(jax.ShapeDtypeStruct((4, 160, 128), BF16),
                    jax.ShapeDtypeStruct((ng, 4, width), F32)),
-        in_specs=[vmem, pl.BlockSpec(memory_space=pl.ANY), pl.BlockSpec(memory_space=pltpu.SMEM),
-                  vmem, vmem, vmem],
+        in_specs=[pl.BlockSpec(memory_space=pltpu.HBM)] * 6,
         out_specs=(pl.BlockSpec(memory_space=pl.ANY), vmem),
         scratch_shapes=[
+            pltpu.VMEM((4, mloc, 2, ncoef), BF16),
+            pltpu.SMEM((mloc,), jnp.int32),
+            pltpu.VMEM((nnz // eb, eb), jnp.int32),
+            pltpu.VMEM((nnz, BLOCK), BF16),
+            pltpu.VMEM((nnz // eb, eb), jnp.int32),
             pltpu.VMEM((mloc, ncoef, lats), BF16),
             pltpu.VMEM((nw, 2, 128), BF16),
             pltpu.VMEM((nw, 2, 128), BF16),
@@ -277,13 +308,16 @@
             pltpu.VMEM((nw, 128), F32),
             pltpu.VMEM((ng, 4, width), F32),
             pltpu.VMEM((ng, 4, width), F32),
-            pltpu.VMEM((320, 2 * mloc * nw), BF16),
-            pltpu.VMEM((2 * mloc * nw, 256), BF16),
+            pltpu.VMEM((320, 2560), BF16),
+            pltpu.VMEM((2560, 256), BF16),
+            pltpu.VMEM((10, 80, 128), F32),
+            pltpu.VMEM((10, 80, 128), F32),
             pltpu.VMEM((144, nq), BF16),
-            pltpu.VMEM((nq, BPW), BF16),
+            pltpu.VMEM((nq, 128), BF16),
             pltpu.VMEM((128, nw), F32),
             pltpu.VMEM((4, 160, 128), BF16),
             pltpu.VMEM((nnz, nq), BF16),
+            pltpu.SemaphoreType.DMA((5,)),
             pltpu.SemaphoreType.DMA((mloc,)),
             pltpu.SemaphoreType.DMA,
             pltpu.SemaphoreType.DMA,
@@ -295,9 +329,10 @@
         ],
         compiler_params=pltpu.CompilerParams(
             collective_id=0, has_side_effects=True, vmem_limit_bytes=40 * 1024 * 1024),
-    )(jnp.transpose(spectra, (0, 2, 1, 3)), legendre, wave_numbers,
-      block_index.reshape(nnz // eb, eb), block_weights.reshape(nnz, BLOCK),
-      basin_index.reshape(nnz // eb, eb))
+    )(*[pltpu.with_memory_space_constraint(x, pltpu.HBM) for x in (
+        jnp.transpose(spectra, (0, 2, 1, 3)), legendre, wave_numbers,
+        block_index.reshape(nnz // eb, eb), block_weights.reshape(nnz, BLOCK),
+        basin_index.reshape(nnz // eb, eb))])
     grid = jnp.transpose(grid.reshape(4, 80, 2, 128), (0, 2, 1, 3)).reshape(4, 2, 1, NLON)
     return grid, sums.reshape(ng * 4, width)
 

time: 57.6 us -> 44.5 us (0.77)
  Pallas kernels: 49.5 us -> 42.5 us
  local copies, waits for them, and re-layouts: 7.09 us -> 1.27 us
    pallas_call x1, Pallas kernels: 49.5 us -> 42.5 us  [per_device(): pl.pallas_call(functools.partial(kernel, nw, ng), out_shape=(jax.ShapeDty...]
    unnamed x14 -> x2, local copies, waits for them, and re-layouts: 7.09 us -> 1.27 us
where the time goes in v2:
time: 44.5 us; the launch traced here: 44.4 us
  Pallas kernels  42.5 us (96%)
  local copies, waits for them, and re-layouts  1.27 us (3%)
  between operations  0.64 us (1%)
    pallas_call x1, Pallas kernels, per_device(): pl.pallas_call(functools.partial(kernel, nw, ng), out_shape=(jax.ShapeDty...  42.5 us
    unnamed x2, local copies, waits for them, and re-layouts  1.27 us

profile of v2, /device:TPU:1, one launch (start us, length us, event | category | flops | bytes accessed | tf_op | source)
XLA Modules:
  0.0 44.4 jit_solution(13449728979782254463)
XLA Ops:
  0.6 42.5 %shard_map.77 = (bf16[4,160,128]{2,1,0:T(8,128)(2,1)S(1)}, f32[4,4,128]{2,1,0:T(4,128)S(1)}) custom-call(bf16[4,10,2,1280]{3,2,1,0:T(2,128)(2,1)} %bitcast.13, bf16[10,1280,128]{2,1,0:T(8,128)(2,1)} %leg_hbm.1, s32[10]{0:T(128)} %wn_hbm.1, s32[8,128]{1,0:T(8,128)} %bitcast.14, bf16[1024,128]{1,0:T(8,128)(2,1)} %bitcast.12, s32[8,128]{1,0:T(8,128)} %bitcast.15), custom_call_target="tpu_custom_call" | custom-call | tf_op jit(solution)/shard_map/pallas_call | solution.py:292
  43.1 0.7 %copy.11 = bf16[4,2,1,10240]{3,1,2,0:T(2,128)(2,1)} copy(bf16[4,2,1,10240]{3,1,2,0:T(2,128)(2,1)S(1)} %bitcast.10) | data formatting | bytes 327680
  43.8 0.6 %copy.12 = f32[16,128]{1,0:T(8,128)} copy(f32[16,128]{1,0:T(8,128)S(1)} %bitcast.11) | data formatting | bytes 16384

commit v3 on v2

--- a/solution.py
+++ b/solution.py
@@ -60,8 +60,8 @@
 
 def kernel(nw, ng, spec_hbm, leg_hbm, wn_hbm, blk_hbm, wgt_hbm, bas_hbm,
            grid_hbm, sums_ref,
-           spec_ref, wn_ref, blk_ref, wgt_ref, bas_ref, leg, sa, ra, sb, rb, sd, rd, tu, ba, ca, sn, ws, one, vs, gr, pm,
-           in_sem, leg_sem, grid_sem, sa_sem, ra_sem, sb_sem, rb_sem, sd_sem, rd_sem):
+           spec_ref, wn_ref, blk_ref, wgt_ref, bas_ref, leg, sa, ra, rz, sb, rb, sd, rd, tu, ba, ca, sn, ws, one, vs, gr, pm,
+           in_sem, leg_sem, grid_sem, sa_sem, ra_sem, sz_sem, rz_sem, sb_sem, rb_sem, sd_sem, rd_sem):
     me, y = lax.axis_index("wave"), lax.axis_index("basin")
     mloc = leg.shape[0]
     nb, eb = bas_ref.shape
@@ -72,7 +72,14 @@
     def greet(to):
         pl.semaphore_signal(barrier, inc=1, device_id=(to, y), device_id_type=MESH)
 
-    each_other(me, nw, greet)
+    @pl.when(me != 0)
+    def _():
+        each_other(me, nw, greet)
+
+    @pl.when(me == 0)
+    def _():
+        greet(1)
+
     for k in range(1, ng):
         pl.semaphore_signal(barrier, inc=1, device_id=(me, lax.rem(y + k, ng)), device_id_type=MESH)
 
@@ -142,12 +149,20 @@
     part_im = ordered[:, 128:] + where_to
     sa[...] = jnp.concatenate([part_re[:, None, :], part_im[:, None, :]], axis=1).astype(BF16)
 
-    pl.semaphore_wait(barrier, nw - 1 + ng - 1)
+    pl.semaphore_wait(barrier, nw - 1 + ng - 1 - (me > 1).astype(jnp.int32))
+
+    @pl.when(me > 1)
+    def _():
+        pltpu.make_async_remote_copy(
+            src_ref=sa.at[pl.ds(0, 1)], dst_ref=rz.at[pl.ds(me, 1)], send_sem=sz_sem,
+            recv_sem=rz_sem, device_id=(1, y), device_id_type=MESH).start()
 
     def send_a(to):
-        pltpu.make_async_remote_copy(
-            src_ref=sa.at[pl.ds(to, 1)], dst_ref=ra.at[pl.ds(me, 1)], send_sem=sa_sem,
-            recv_sem=ra_sem, device_id=(to, y), device_id_type=MESH).start()
+        @pl.when(to != 0)
+        def _():
+            pltpu.make_async_remote_copy(
+                src_ref=sa.at[pl.ds(to, 1)], dst_ref=ra.at[pl.ds(me, 1)], send_sem=sa_sem,
+                recv_sem=ra_sem, device_id=(to, y), device_id_type=MESH).start()
 
     each_other(me, nw, send_a)
     ra[pl.ds(me, 1)] = sa[pl.ds(me, 1)]
@@ -185,6 +200,16 @@
         ba[hi * 256:hi * 256 + 128, 128:] = (cos_b * flip).astype(BF16)
         ba[hi * 256 + 128:hi * 256 + 256, :128] = (-sin_b).astype(BF16)
         ba[hi * 256 + 128:hi * 256 + 256, 128:] = (-sin_b * flip).astype(BF16)
+
+    pass_on = pltpu.make_async_remote_copy(
+        src_ref=rz.at[pl.ds(1, nw - 1)], dst_ref=ra.at[pl.ds(1, nw - 1)], send_sem=sz_sem,
+        recv_sem=ra_sem, device_id=(0, y), device_id_type=MESH)
+
+    @pl.when(me == 1)
+    def _():
+        rz[1] = sa[0]
+        pltpu.make_async_copy(sa.at[pl.ds(0, nw - 2)], rz.at[pl.ds(0, nw - 2)], rz_sem).wait()
+        pass_on.start()
 
     pltpu.make_async_copy(sa.at[pl.ds(0, nw - 1)], ra.at[pl.ds(0, nw - 1)], ra_sem).wait()
 
@@ -276,7 +301,22 @@
     sums_ref[...] = rd[...]
 
     out.wait()
-    pltpu.make_async_copy(sa.at[pl.ds(0, nw - 1)], ra.at[pl.ds(0, nw - 1)], sa_sem).wait()
+    @pl.when(me == 0)
+    def _():
+        pltpu.make_async_copy(sa.at[pl.ds(0, nw - 1)], ra.at[pl.ds(0, nw - 1)], sa_sem).wait()
+
+    @pl.when(me != 0)
+    def _():
+        pltpu.make_async_copy(sa.at[pl.ds(0, nw - 2)], ra.at[pl.ds(0, nw - 2)], sa_sem).wait()
+
+    @pl.when(me == 1)
+    def _():
+        pass_on.wait_send()
+
+    @pl.when(me > 1)
+    def _():
+        pltpu.make_async_copy(sa.at[pl.ds(0, 1)], rz.at[pl.ds(0, 1)], sz_sem).wait()
+
     pltpu.make_async_copy(sb.at[pl.ds(0, nw - 1)], rb.at[pl.ds(0, nw - 1)], sb_sem).wait()
     pltpu.make_async_copy(sd.at[pl.ds(0, ng - 1)], rd.at[pl.ds(0, ng - 1)], sd_sem).wait()
 
@@ -304,6 +344,7 @@
             pltpu.VMEM((mloc, ncoef, lats), BF16),
             pltpu.VMEM((nw, 2, 128), BF16),
             pltpu.VMEM((nw, 2, 128), BF16),
+            pltpu.VMEM((nw, 2, 128), BF16),
             pltpu.VMEM((nw, 128), F32),
             pltpu.VMEM((nw, 128), F32),
             pltpu.VMEM((ng, 4, width), F32),
@@ -326,6 +367,8 @@
             pltpu.SemaphoreType.DMA,
             pltpu.SemaphoreType.DMA,
             pltpu.SemaphoreType.DMA,
+            pltpu.SemaphoreType.DMA,
+            pltpu.SemaphoreType.DMA,
         ],
         compiler_params=pltpu.CompilerParams(
             collective_id=0, has_side_effects=True, vmem_limit_bytes=40 * 1024 * 1024),

time: 44.5 us -> 44.3 us (level)
  no operation moved by 1% of the time
where the time goes in v3:
time: 44.3 us; the launch traced here: 44.1 us
  Pallas kernels  42.2 us (95%)
  local copies, waits for them, and re-layouts  1.27 us (3%)
  between operations  0.64 us (1%)
    pallas_call x1, Pallas kernels, per_device(): pl.pallas_call(functools.partial(kernel, nw, ng), out_shape=(jax.ShapeDty...  42.2 us
    unnamed x2, local copies, waits for them, and re-layouts  1.27 us

profile of v3, /device:TPU:1, one launch (start us, length us, event | category | flops | bytes accessed | tf_op | source)
XLA Modules:
  0.0 44.1 jit_solution(4867228581450767136)
XLA Ops:
  0.6 42.2 %shard_map.77 = (bf16[4,160,128]{2,1,0:T(8,128)(2,1)S(1)}, f32[4,4,128]{2,1,0:T(4,128)S(1)}) custom-call(bf16[4,10,2,1280]{3,2,1,0:T(2,128)(2,1)} %bitcast.13, bf16[10,1280,128]{2,1,0:T(8,128)(2,1)} %leg_hbm.1, s32[10]{0:T(128)} %wn_hbm.1, s32[8,128]{1,0:T(8,128)} %bitcast.14, bf16[1024,128]{1,0:T(8,128)(2,1)} %bitcast.12, s32[8,128]{1,0:T(8,128)} %bitcast.15), custom_call_target="tpu_custom_call" | custom-call | tf_op jit(solution)/shard_map/pallas_call | solution.py:332
  42.9 0.7 %copy.11 = bf16[4,2,1,10240]{3,1,2,0:T(2,128)(2,1)} copy(bf16[4,2,1,10240]{3,1,2,0:T(2,128)(2,1)S(1)} %bitcast.10) | data formatting | bytes 327680
  43.5 0.6 %copy.12 = f32[16,128]{1,0:T(8,128)} copy(f32[16,128]{1,0:T(8,128)S(1)} %bitcast.11) | data formatting | bytes 16384

commit v4 on v2

--- a/solution.py
+++ b/solution.py
@@ -60,7 +60,7 @@
 
 def kernel(nw, ng, spec_hbm, leg_hbm, wn_hbm, blk_hbm, wgt_hbm, bas_hbm,
            grid_hbm, sums_ref,
-           spec_ref, wn_ref, blk_ref, wgt_ref, bas_ref, leg, sa, ra, sb, rb, sd, rd, tu, ba, ca, sn, ws, one, vs, gr, pm,
+           spec_ref, wn_ref, blk_ref, wgt_ref, bas_ref, leg, sa, ra, sb, rb, sd, rd, tu, ba, ca, sn, ws, key, one, vs, gr, pm,
            in_sem, leg_sem, grid_sem, sa_sem, ra_sem, sb_sem, rb_sem, sd_sem, rd_sem):
     me, y = lax.axis_index("wave"), lax.axis_index("basin")
     mloc = leg.shape[0]
@@ -136,8 +136,9 @@
     bring[2].wait()
     for m in range(mloc):
         wn = wn_ref[m]
-        numbers = numbers + jnp.where(lane == 80 + m, (wn >> 7).astype(F32), 0.0)
-        numbers = numbers + jnp.where(lane == 96 + m, (wn & 127).astype(F32), 0.0)
+        chunk = (wn & 1) * 5 + (wn >> 8)
+        numbers = numbers + jnp.where(lane == 80 + m, chunk.astype(F32), 0.0)
+        numbers = numbers + jnp.where(lane == 96 + m, ((wn >> 1) & 127).astype(F32), 0.0)
     part_re = ordered[:, :128] + numbers
     part_im = ordered[:, 128:] + where_to
     sa[...] = jnp.concatenate([part_re[:, None, :], part_im[:, None, :]], axis=1).astype(BF16)
@@ -168,23 +169,35 @@
                 col == spot, 1.0, 0.0).astype(BF16)
     qc = min(256, nq)
     for c in range(nq // qc):
-        ws[:, c * qc:(c + 1) * qc] = jnp.dot(
-            left, pm[:, c * qc:(c + 1) * qc], preferred_element_type=F32).astype(BF16)
-
-    a_of = (iota((80, 128), 0) >> 1).astype(F32)
+        cols = slice(c * qc, (c + 1) * qc)
+        slots = jnp.dot(left, pm[:, cols], preferred_element_type=F32)
+        block = slots[128:129]
+        south = jnp.where(block >= 80.0, 1.0, 0.0)
+        a = block - 80.0 * south
+        side = jnp.where(a >= 40.0, 1.0, 0.0)
+        ws[:128, cols] = jnp.where(side == 0.0, slots[:128], 0.0).astype(BF16)
+        ws[128:, cols] = jnp.where(side == 1.0, slots[:128], 0.0).astype(BF16)
+        key[:, cols] = jnp.broadcast_to((a - 40.0 * side) * 2.0 + south, (8, qc))
+
+    a_of = (iota((40, 128), 0) >> 1).astype(F32)
     lane_of = iota((1, 128), 1).astype(F32)
     m_of, b_of = iota((128, LB), 0).astype(F32), iota((128, LB), 1).astype(F32)
     flip = 1.0 - 2.0 * (iota((128, LB), 0) & 1).astype(F32)
-    for hi in range(10):
-        number = lane_of + 128.0 * hi
+    for k in range(10):
+        first = 256.0 * (k % 5) + k // 5
+        number = 2.0 * lane_of + first
         weight = jnp.where(number == 0.0, 1.0, 2.0)
         cos_a, sin_a = cos_sin(number * a_of, 80.0)
-        ca[hi], sn[hi] = cos_a * weight, sin_a * weight
-        cos_b, sin_b = cos_sin((m_of + 128.0 * hi) * b_of, float(NLON))
-        ba[hi * 256:hi * 256 + 128, :128] = cos_b.astype(BF16)
-        ba[hi * 256:hi * 256 + 128, 128:] = (cos_b * flip).astype(BF16)
-        ba[hi * 256 + 128:hi * 256 + 256, :128] = (-sin_b).astype(BF16)
-        ba[hi * 256 + 128:hi * 256 + 256, 128:] = (-sin_b * flip).astype(BF16)
+        ca[k], sn[k] = cos_a * weight, sin_a * weight
+        cos_b, sin_b = cos_sin((2.0 * m_of + first) * b_of, float(NLON))
+        ba[k * 256:k * 256 + 128, :128] = cos_b.astype(BF16)
+        ba[k * 256 + 128:k * 256 + 256, :128] = (-sin_b).astype(BF16)
+        if k < 5:
+            ba[k * 256:k * 256 + 128, 128:] = (cos_b * flip).astype(BF16)
+            ba[k * 256 + 128:k * 256 + 256, 128:] = (-sin_b * flip).astype(BF16)
+        else:
+            ba[k * 256:k * 256 + 128, 128:] = (-sin_b * flip).astype(BF16)
+            ba[k * 256 + 128:k * 256 + 256, 128:] = (-cos_b * flip).astype(BF16)
 
     pltpu.make_async_copy(sa.at[pl.ds(0, nw - 1)], ra.at[pl.ds(0, nw - 1)], ra_sem).wait()
 
@@ -203,31 +216,35 @@
                       preferred_element_type=F32)
 
     parity = (iota((8, 128), 0) & 1) == 0
-    for hi in range(10):
-        cos_a, sin_a = ca[hi].reshape(10, 8, 128), sn[hi].reshape(10, 8, 128)
-        g_re, g_im = columns[hi * 16:hi * 16 + 8], columns[hi * 16 + 8:hi * 16 + 16]
+    for k in range(10):
+        cos_a, sin_a = ca[k].reshape(5, 8, 128), sn[k].reshape(5, 8, 128)
+        g_re, g_im = columns[k * 16:k * 16 + 8], columns[k * 16 + 8:k * 16 + 16]
         for f in range(4):
             fr = jnp.where(parity, g_re[2 * f:2 * f + 1], g_re[2 * f + 1:2 * f + 2])[None]
             fi = jnp.where(parity, g_im[2 * f:2 * f + 1], g_im[2 * f + 1:2 * f + 2])[None]
-            t_re = (fr * cos_a - fi * sin_a).reshape(80, 128)
-            t_im = (fr * sin_a + fi * cos_a).reshape(80, 128)
-            tu[f * 80:(f + 1) * 80, hi * 256:hi * 256 + 128] = t_re.astype(BF16)
-            tu[f * 80:(f + 1) * 80, hi * 256 + 128:hi * 256 + 256] = t_im.astype(BF16)
+            t_re = (fr * cos_a - fi * sin_a).reshape(40, 128)
+            t_im = (fr * sin_a + fi * cos_a).reshape(40, 128)
+            tu[k // 5, f * 40:(f + 1) * 40, k % 5 * 256:k % 5 * 256 + 128] = t_re.astype(BF16)
+            tu[k // 5, f * 40:(f + 1) * 40, k % 5 * 256 + 128:k % 5 * 256 + 256] = t_im.astype(BF16)
     scale = 1.0 / math.sqrt(2.0 * mloc * nw)
-    lines = jnp.dot(tu[...], ba[...], preferred_element_type=F32) * scale
+    even = jnp.dot(tu[0], ba[:1280], preferred_element_type=F32)
+    odd = jnp.dot(tu[1], ba[1280:], preferred_element_type=F32)
+    plus, minus = (even + odd) * scale, (even - odd) * scale
     for f in range(4):
-        gr[f, :80] = lines[f * 80:(f + 1) * 80, :128].astype(BF16)
-        gr[f, 80:] = lines[f * 80:(f + 1) * 80, 128:].astype(BF16)
-
-    row = iota((160, qc), 0)
-    block_of = (row & 1) * 80 + (row >> 1)
-    block_of = block_of.astype(F32)
+        rows = slice(f * 40, (f + 1) * 40)
+        for side, lines in enumerate((plus, minus)):
+            gr[f, side * 80:(side + 1) * 80] = jnp.concatenate(
+                [lines[rows, :128], lines[rows, 128:]], axis=0).astype(BF16)
+
+    row = iota((80, qc), 0).astype(F32)
+    sides = jnp.concatenate(
+        [jnp.concatenate([gr[f, :80], gr[f, 80:]], axis=1) for f in range(4)], axis=0)
     for c in range(nq // qc):
         cols = slice(c * qc, (c + 1) * qc)
-        hit = block_of == ws[128:129, cols].astype(F32)
-        prod = jnp.dot(gr[...].reshape(640, 128), ws[:128, cols], preferred_element_type=F32)
+        hit = row == key[0:1, cols]
+        prod = jnp.dot(sides, ws[:, cols], preferred_element_type=F32)
         val = jnp.concatenate(
-            [jnp.sum(jnp.where(hit, prod[f * 160:(f + 1) * 160], 0.0), axis=0, keepdims=True)
+            [jnp.sum(jnp.where(hit, prod[f * 80:(f + 1) * 80], 0.0), axis=0, keepdims=True)
              for f in range(4)], axis=0)
         high = val.astype(BF16).astype(F32)
         val = jnp.concatenate([high, val - high], axis=0)
@@ -308,11 +325,12 @@
             pltpu.VMEM((nw, 128), F32),
             pltpu.VMEM((ng, 4, width), F32),
             pltpu.VMEM((ng, 4, width), F32),
-            pltpu.VMEM((320, 2560), BF16),
+            pltpu.VMEM((2, 160, 1280), BF16),
             pltpu.VMEM((2560, 256), BF16),
-            pltpu.VMEM((10, 80, 128), F32),
-            pltpu.VMEM((10, 80, 128), F32),
-            pltpu.VMEM((144, nq), BF16),
+            pltpu.VMEM((10, 40, 128), F32),
+            pltpu.VMEM((10, 40, 128), F32),
+            pltpu.VMEM((256, nq), BF16),
+            pltpu.VMEM((8, nq), F32),
             pltpu.VMEM((nq, 128), BF16),
             pltpu.VMEM((128, nw), F32),
             pltpu.VMEM((4, 160, 128), BF16),

time: 44.5 us -> 43.7 us (0.982)
  Pallas kernels: 42.5 us -> 41.7 us
    pallas_call x1, Pallas kernels: 42.5 us -> 41.7 us  [per_device(): pl.pallas_call(functools.partial(kernel, nw, ng), out_shape=(jax.ShapeDty...]
where the time goes in v4:
time: 43.7 us; the launch traced here: 43.6 us
  Pallas kernels  41.7 us (95%)
  local copies, waits for them, and re-layouts  1.27 us (3%)
  between operations  0.64 us (1%)
    pallas_call x1, Pallas kernels, per_device(): pl.pallas_call(functools.partial(kernel, nw, ng), out_shape=(jax.ShapeDty...  41.7 us
    unnamed x2, local copies, waits for them, and re-layouts  1.27 us

profile of v4, /device:TPU:1, one launch (start us, length us, event | category | flops | bytes accessed | tf_op | source)
XLA Modules:
  0.0 43.6 jit_solution(1737886725377260887)
XLA Ops:
  0.6 41.7 %shard_map.77 = (bf16[4,160,128]{2,1,0:T(8,128)(2,1)S(1)}, f32[4,4,128]{2,1,0:T(4,128)S(1)}) custom-call(bf16[4,10,2,1280]{3,2,1,0:T(2,128)(2,1)} %bitcast.13, bf16[10,1280,128]{2,1,0:T(8,128)(2,1)} %leg_hbm.1, s32[10]{0:T(128)} %wn_hbm.1, s32[8,128]{1,0:T(8,128)} %bitcast.14, bf16[1024,128]{1,0:T(8,128)(2,1)} %bitcast.12, s32[8,128]{1,0:T(8,128)} %bitcast.15), custom_call_target="tpu_custom_call" | custom-call | tf_op jit(solution)/shard_map/pallas_call | solution.py:309
  42.3 0.7 %copy.11 = bf16[4,2,1,10240]{3,1,2,0:T(2,128)(2,1)} copy(bf16[4,2,1,10240]{3,1,2,0:T(2,128)(2,1)S(1)} %bitcast.10) | data formatting | bytes 327680
  43.0 0.6 %copy.12 = f32[16,128]{1,0:T(8,128)} copy(f32[16,128]{1,0:T(8,128)S(1)} %bitcast.11) | data formatting | bytes 16384

commit v5 on v4

--- a/solution.py
+++ b/solution.py
@@ -60,7 +60,7 @@
 
 def kernel(nw, ng, spec_hbm, leg_hbm, wn_hbm, blk_hbm, wgt_hbm, bas_hbm,
            grid_hbm, sums_ref,
-           spec_ref, wn_ref, blk_ref, wgt_ref, bas_ref, leg, sa, ra, sb, rb, sd, rd, tu, ba, ca, sn, ws, key, one, vs, gr, pm,
+           spec_ref, wn_ref, blk_ref, wgt_ref, bas_ref, leg, sa, ra, sb, rb, sd, rd, tu, ba, ca, sn, ws, key, one, vs, gr, spread, sm,
            in_sem, leg_sem, grid_sem, sa_sem, ra_sem, sb_sem, rb_sem, sd_sem, rd_sem):
     me, y = lax.axis_index("wave"), lax.axis_index("basin")
     mloc = leg.shape[0]
@@ -115,13 +115,17 @@
     ncoef = spec_ref.shape[3]
     odd = lax.rem(iota((8, ncoef), 1), 2) == 1
     bring[1].wait()
-    sums = []
-    for m in range(mloc):
+
+    def column(m, carry):
         rows = jnp.concatenate([spec_ref[f, m].astype(F32) for f in range(4)], axis=0)
         both = jnp.concatenate([rows, jnp.where(odd, -rows, rows)], axis=0).astype(BF16)
         pltpu.make_async_copy(leg_hbm.at[m], leg.at[m], leg_sem.at[m]).wait()
-        sums.append(jnp.dot(both, leg[m], preferred_element_type=F32))
-    sums = jnp.concatenate(sums, axis=0)
+        sm[pl.ds(pl.multiple_of(m * 16, 16), 16)] = jnp.dot(
+            both, leg[m], preferred_element_type=F32)
+        return carry
+
+    lax.fori_loop(0, mloc, column, 0)
+    sums = sm[...]
     if mloc * 16 % 128:
         sums = jnp.concatenate([sums, jnp.zeros((256 - mloc * 16, nw), F32)], axis=0)
     by_lat = jnp.transpose(sums).astype(BF16)
@@ -161,16 +165,15 @@
     turned_w = jnp.concatenate(
         [jnp.transpose(wgt_ref[i * eb:(i + 1) * eb].astype(F32)) for i in range(nb)], axis=1)
     left = jnp.concatenate([turned_w, ext], axis=0).astype(BF16)
+    qc = min(256, nq)
     for i in range(nb):
-        col = jnp.broadcast_to(place_cols[:, i:i + 1], (eb, 128 if nq >= 128 else nq))
-        for c in range(max(1, nq // 128)):
-            spot = (iota(col.shape, 1) + c * 128).astype(F32)
-            pm[i * eb:(i + 1) * eb, c * 128:c * 128 + col.shape[1]] = jnp.where(
-                col == spot, 1.0, 0.0).astype(BF16)
-    qc = min(256, nq)
-    for c in range(nq // qc):
-        cols = slice(c * qc, (c + 1) * qc)
-        slots = jnp.dot(left, pm[:, cols], preferred_element_type=F32)
+        spread[i * eb:(i + 1) * eb] = jnp.broadcast_to(place_cols[:, i:i + 1], (eb, qc))
+    spot = iota((1, qc), 1).astype(F32)
+
+    def put(c, carry):
+        cols = pl.ds(pl.multiple_of(c * qc, qc), qc)
+        placed = jnp.where(spread[...] == spot + (c * qc).astype(F32), 1.0, 0.0).astype(BF16)
+        slots = jnp.dot(left, placed, preferred_element_type=F32)
         block = slots[128:129]
         south = jnp.where(block >= 80.0, 1.0, 0.0)
         a = block - 80.0 * south
@@ -178,42 +181,49 @@
         ws[:128, cols] = jnp.where(side == 0.0, slots[:128], 0.0).astype(BF16)
         ws[128:, cols] = jnp.where(side == 1.0, slots[:128], 0.0).astype(BF16)
         key[:, cols] = jnp.broadcast_to((a - 40.0 * side) * 2.0 + south, (8, qc))
+        return carry
+
+    lax.fori_loop(0, nq // qc, put, 0)
 
     a_of = (iota((40, 128), 0) >> 1).astype(F32)
     lane_of = iota((1, 128), 1).astype(F32)
     m_of, b_of = iota((128, LB), 0).astype(F32), iota((128, LB), 1).astype(F32)
     flip = 1.0 - 2.0 * (iota((128, LB), 0) & 1).astype(F32)
-    for k in range(10):
-        first = 256.0 * (k % 5) + k // 5
+
+    def table(k, carry):
+        is_odd = k >= 5
+        odd_one = is_odd.astype(jnp.int32)
+        first = ((k - 5 * odd_one) * 256 + odd_one).astype(F32)
         number = 2.0 * lane_of + first
         weight = jnp.where(number == 0.0, 1.0, 2.0)
         cos_a, sin_a = cos_sin(number * a_of, 80.0)
         ca[k], sn[k] = cos_a * weight, sin_a * weight
         cos_b, sin_b = cos_sin((2.0 * m_of + first) * b_of, float(NLON))
-        ba[k * 256:k * 256 + 128, :128] = cos_b.astype(BF16)
-        ba[k * 256 + 128:k * 256 + 256, :128] = (-sin_b).astype(BF16)
-        if k < 5:
-            ba[k * 256:k * 256 + 128, 128:] = (cos_b * flip).astype(BF16)
-            ba[k * 256 + 128:k * 256 + 256, 128:] = (-sin_b * flip).astype(BF16)
-        else:
-            ba[k * 256:k * 256 + 128, 128:] = (-sin_b * flip).astype(BF16)
-            ba[k * 256 + 128:k * 256 + 256, 128:] = (-cos_b * flip).astype(BF16)
+        row = pl.multiple_of(k * 256, 256)
+        ba[pl.ds(row, 128), :128] = cos_b.astype(BF16)
+        ba[pl.ds(row + 128, 128), :128] = (-sin_b).astype(BF16)
+        ba[pl.ds(row, 128), 128:] = (jnp.where(is_odd, -sin_b, cos_b) * flip).astype(BF16)
+        ba[pl.ds(row + 128, 128), 128:] = (jnp.where(is_odd, -cos_b, -sin_b) * flip).astype(BF16)
+        return carry
+
+    lax.fori_loop(0, 10, table, 0)
 
     pltpu.make_async_copy(sa.at[pl.ds(0, nw - 1)], ra.at[pl.ds(0, nw - 1)], ra_sem).wait()
 
     got = ra[...].astype(F32)
     re, im = got[:, 0, :], got[:, 1, :]
     re_t, im_t = jnp.transpose(re), jnp.transpose(im)
-    low_lane = iota((nw, 128), 1).astype(F32)
+    low_row = iota((128, nw), 0).astype(F32)
     lefts, rights = [], []
     for m in range(mloc):
         both = jnp.concatenate([re_t[m * 8:(m + 1) * 8], im_t[m * 8:(m + 1) * 8]], axis=0)
         high = re_t[80 + m:81 + m]
         lefts.append(jnp.concatenate(
             [jnp.where(high == float(hi), both, 0.0) for hi in range(10)], axis=0).astype(BF16))
-        rights.append(jnp.where(re[:, 96 + m:97 + m] == low_lane, 1.0, 0.0).astype(BF16))
-    columns = jnp.dot(jnp.concatenate(lefts, axis=1), jnp.concatenate(rights, axis=0),
-                      preferred_element_type=F32)
+        rights.append(jnp.where(re_t[96 + m:97 + m] == low_row, 1.0, 0.0).astype(BF16))
+    columns = lax.dot_general(
+        jnp.concatenate(lefts, axis=1), jnp.concatenate(rights, axis=1), (((1,), (1,)), ((), ())),
+        preferred_element_type=F32)
 
     parity = (iota((8, 128), 0) & 1) == 0
     for k in range(10):
@@ -264,8 +274,8 @@
     out.start()
 
     for s in range(SLOTS):
-        one[s * nw:(s + 1) * nw] = jnp.where(
-            im[:, 112 + s:113 + s] == low_lane, 1.0, 0.0).astype(BF16)
+        one[:, s * nw:(s + 1) * nw] = jnp.where(
+            im_t[112 + s:113 + s] == low_row, 1.0, 0.0).astype(BF16)
 
     pltpu.make_async_copy(sb.at[pl.ds(0, nw - 1)], rb.at[pl.ds(0, nw - 1)], rb_sem).wait()
     val = jnp.transpose(rb[...])
@@ -275,14 +285,15 @@
         named.append(jnp.concatenate(
             [jnp.where(high == float(hi), val[s * 8:(s + 1) * 8], 0.0) for hi in range(BPW // 128)],
             axis=0).astype(BF16))
-    dense = jnp.dot(jnp.concatenate(named, axis=1), one[...], preferred_element_type=F32)
+    dense = lax.dot_general(jnp.concatenate(named, axis=1), one[...], (((1,), (1,)), ((), ())),
+                            preferred_element_type=F32)
     dense = [dense[hi * 8:hi * 8 + 4] + dense[hi * 8 + 4:hi * 8 + 8] for hi in range(BPW // 128)]
     each = BPW // 128 // ng
     for g in range(ng):
         for k in range(each):
             sd[g, :, k * 128:(k + 1) * 128] = dense[g * each + k]
     moves = []
-    for k in range(1, ng):
+    for k in sorted(range(1, ng), key=lambda k: abs(2 * k - ng)):
         to = lax.rem(y + k, ng)
         moves.append(pltpu.make_async_remote_copy(
             src_ref=sd.at[to], dst_ref=rd.at[y], send_sem=sd_sem, recv_sem=rd_sem,
@@ -331,10 +342,11 @@
             pltpu.VMEM((10, 40, 128), F32),
             pltpu.VMEM((256, nq), BF16),
             pltpu.VMEM((8, nq), F32),
-            pltpu.VMEM((nq, 128), BF16),
+            pltpu.VMEM((128, nq), BF16),
             pltpu.VMEM((128, nw), F32),
             pltpu.VMEM((4, 160, 128), BF16),
-            pltpu.VMEM((nnz, nq), BF16),
+            pltpu.VMEM((nnz, min(256, nq)), F32),
+            pltpu.VMEM((16 * mloc, nw), F32),
             pltpu.SemaphoreType.DMA((5,)),
             pltpu.SemaphoreType.DMA((mloc,)),
             pltpu.SemaphoreType.DMA,

time: 43.7 us -> 42.6 us (0.975)
  Pallas kernels: 41.7 us -> 40.5 us
    pallas_call x1, Pallas kernels: 41.7 us -> 40.5 us  [per_device(): pl.pallas_call(functools.partial(kernel, nw, ng), out_shape=(jax.ShapeDty...]
where the time goes in v5:
time: 42.6 us; the launch traced here: 42.4 us
  Pallas kernels  40.5 us (95%)
  local copies, waits for them, and re-layouts  1.27 us (3%)
  between operations  0.64 us (2%)
    pallas_call x1, Pallas kernels, per_device(): pl.pallas_call(functools.partial(kernel, nw, ng), out_shape=(jax.ShapeDty...  40.5 us
    unnamed x2, local copies, waits for them, and re-layouts  1.27 us

profile of v5, /device:TPU:1, one launch (start us, length us, event | category | flops | bytes accessed | tf_op | source)
XLA Modules:
  0.0 42.4 jit_solution(11300605713530362713)
XLA Ops:
  0.6 40.5 %shard_map.77 = (bf16[4,160,128]{2,1,0:T(8,128)(2,1)S(1)}, f32[4,4,128]{2,1,0:T(4,128)S(1)}) custom-call(bf16[4,10,2,1280]{3,2,1,0:T(2,128)(2,1)} %bitcast.13, bf16[10,1280,128]{2,1,0:T(8,128)(2,1)} %leg_hbm.1, s32[10]{0:T(128)} %wn_hbm.1, s32[8,128]{1,0:T(8,128)} %bitcast.14, bf16[1024,128]{1,0:T(8,128)(2,1)} %bitcast.12, s32[8,128]{1,0:T(8,128)} %bitcast.15), custom_call_target="tpu_custom_call" | custom-call | tf_op jit(solution)/shard_map/pallas_call | solution.py:320
  41.2 0.7 %copy.11 = bf16[4,2,1,10240]{3,1,2,0:T(2,128)(2,1)} copy(bf16[4,2,1,10240]{3,1,2,0:T(2,128)(2,1)S(1)} %bitcast.10) | data formatting | bytes 327680
  41.8 0.6 %copy.12 = f32[16,128]{1,0:T(8,128)} copy(f32[16,128]{1,0:T(8,128)S(1)} %bitcast.11) | data formatting | bytes 16384

commit v6 on v5

--- a/solution.py
+++ b/solution.py
@@ -49,7 +49,7 @@
             act(plane | there)
         return carry
 
-    lax.fori_loop(0, 15, level, 0)
+    lax.fori_loop(0, 15, level, 0, unroll=5)
     for plane in planes[:-1]:
         act(plane | (z << 1))
 
@@ -59,9 +59,9 @@
 
 
 def kernel(nw, ng, spec_hbm, leg_hbm, wn_hbm, blk_hbm, wgt_hbm, bas_hbm,
-           grid_hbm, sums_ref,
-           spec_ref, wn_ref, blk_ref, wgt_ref, bas_ref, leg, sa, ra, sb, rb, sd, rd, tu, ba, ca, sn, ws, key, one, vs, gr, spread, sm,
-           in_sem, leg_sem, grid_sem, sa_sem, ra_sem, sb_sem, rb_sem, sd_sem, rd_sem):
+           grid_hbm, sums_hbm,
+           spec_ref, wn_ref, blk_ref, wgt_ref, bas_ref, leg, sa, ra, sb, rb, sd, tu, ba, ca, sn, ws, key, one, vs, gr, spread, sm,
+           in_sem, leg_sem, grid_sem, sa_sem, ra_sem, sb_sem, rb_sem, sd_sem, rd_sem, own_sem):
     me, y = lax.axis_index("wave"), lax.axis_index("basin")
     mloc = leg.shape[0]
     nb, eb = bas_ref.shape
@@ -210,8 +210,7 @@
 
     pltpu.make_async_copy(sa.at[pl.ds(0, nw - 1)], ra.at[pl.ds(0, nw - 1)], ra_sem).wait()
 
-    got = ra[...].astype(F32)
-    re, im = got[:, 0, :], got[:, 1, :]
+    re, im = ra[:, 0, :].astype(F32), ra[:, 1, :].astype(F32)
     re_t, im_t = jnp.transpose(re), jnp.transpose(im)
     low_row = iota((128, nw), 0).astype(F32)
     lefts, rights = [], []
@@ -296,17 +295,18 @@
     for k in sorted(range(1, ng), key=lambda k: abs(2 * k - ng)):
         to = lax.rem(y + k, ng)
         moves.append(pltpu.make_async_remote_copy(
-            src_ref=sd.at[to], dst_ref=rd.at[y], send_sem=sd_sem, recv_sem=rd_sem,
+            src_ref=sd.at[to], dst_ref=sums_hbm.at[y], send_sem=sd_sem, recv_sem=rd_sem,
             device_id=(me, to), device_id_type=MESH))
         moves[-1].start()
-    rd[y] = sd[y]
-    pltpu.make_async_copy(sd.at[pl.ds(0, ng - 1)], rd.at[pl.ds(0, ng - 1)], rd_sem).wait()
-    sums_ref[...] = rd[...]
+    own = pltpu.make_async_copy(sd.at[y], sums_hbm.at[y], own_sem)
+    own.start()
+    pltpu.make_async_copy(sd.at[pl.ds(0, ng - 1)], sums_hbm.at[pl.ds(0, ng - 1)], rd_sem).wait()
+    own.wait()
 
     out.wait()
     pltpu.make_async_copy(sa.at[pl.ds(0, nw - 1)], ra.at[pl.ds(0, nw - 1)], sa_sem).wait()
     pltpu.make_async_copy(sb.at[pl.ds(0, nw - 1)], rb.at[pl.ds(0, nw - 1)], sb_sem).wait()
-    pltpu.make_async_copy(sd.at[pl.ds(0, ng - 1)], rd.at[pl.ds(0, ng - 1)], sd_sem).wait()
+    pltpu.make_async_copy(sd.at[pl.ds(0, ng - 1)], sums_hbm.at[pl.ds(0, ng - 1)], sd_sem).wait()
 
 
 def per_device(spectra, legendre, wave_numbers, block_index, block_weights, basin_index):
@@ -316,13 +316,12 @@
     eb = min(128, nnz)
     nq = SLOTS * nw
     width = BPW // ng
-    vmem = pl.BlockSpec(memory_space=pltpu.VMEM)
     grid, sums = pl.pallas_call(
         functools.partial(kernel, nw, ng),
         out_shape=(jax.ShapeDtypeStruct((4, 160, 128), BF16),
                    jax.ShapeDtypeStruct((ng, 4, width), F32)),
         in_specs=[pl.BlockSpec(memory_space=pltpu.HBM)] * 6,
-        out_specs=(pl.BlockSpec(memory_space=pl.ANY), vmem),
+        out_specs=(pl.BlockSpec(memory_space=pl.ANY), pl.BlockSpec(memory_space=pl.ANY)),
         scratch_shapes=[
             pltpu.VMEM((4, mloc, 2, ncoef), BF16),
             pltpu.SMEM((mloc,), jnp.int32),
@@ -334,7 +333,6 @@
             pltpu.VMEM((nw, 2, 128), BF16),
             pltpu.VMEM((nw, 128), F32),
             pltpu.VMEM((nw, 128), F32),
-            pltpu.VMEM((ng, 4, width), F32),
             pltpu.VMEM((ng, 4, width), F32),
             pltpu.VMEM((2, 160, 1280), BF16),
             pltpu.VMEM((2560, 256), BF16),
@@ -356,6 +354,7 @@
             pltpu.SemaphoreType.DMA,
             pltpu.SemaphoreType.DMA,
             pltpu.SemaphoreType.DMA,
+            pltpu.SemaphoreType.DMA,
         ],
         compiler_params=pltpu.CompilerParams(
             collective_id=0, has_side_effects=True, vmem_limit_bytes=40 * 1024 * 1024),

time: 42.6 us -> 42.5 us (level)
  no operation moved by 1% of the time
where the time goes in v6:
time: 42.5 us; the launch traced here: 42.3 us
  Pallas kernels  40.4 us (95%)
  local copies, waits for them, and re-layouts  1.27 us (3%)
  between operations  0.64 us (2%)
    pallas_call x1, Pallas kernels, per_device(): pl.pallas_call(functools.partial(kernel, nw, ng), out_shape=(jax.ShapeDty...  40.4 us
    unnamed x2, local copies, waits for them, and re-layouts  1.27 us

profile of v6, /device:TPU:1, one launch (start us, length us, event | category | flops | bytes accessed | tf_op | source)
XLA Modules:
  0.0 42.3 jit_solution(1708921013093967680)
XLA Ops:
  0.6 40.4 %shard_map.77 = (bf16[4,160,128]{2,1,0:T(8,128)(2,1)S(1)}, f32[4,4,128]{2,1,0:T(4,128)S(1)}) custom-call(bf16[4,10,2,1280]{3,2,1,0:T(2,128)(2,1)} %bitcast.13, bf16[10,1280,128]{2,1,0:T(8,128)(2,1)} %leg_hbm.1, s32[10]{0:T(128)} %wn_hbm.1, s32[8,128]{1,0:T(8,128)} %bitcast.14, bf16[1024,128]{1,0:T(8,128)(2,1)} %bitcast.12, s32[8,128]{1,0:T(8,128)} %bitcast.15), custom_call_target="tpu_custom_call" | custom-call | tf_op jit(solution)/shard_map/pallas_call | solution.py:319
  41.1 0.7 %copy.11 = bf16[4,2,1,10240]{3,1,2,0:T(2,128)(2,1)} copy(bf16[4,2,1,10240]{3,1,2,0:T(2,128)(2,1)S(1)} %bitcast.10) | data formatting | bytes 327680
  41.7 0.6 %copy.12 = f32[16,128]{1,0:T(8,128)} copy(f32[16,128]{1,0:T(8,128)S(1)} %bitcast.11) | data formatting | bytes 16384

commit v7 on v5

--- a/solution.py
+++ b/solution.py
@@ -36,8 +36,9 @@
     return 1.0 - 2.0 * (s * s), 2.0 * (s * c)
 
 
-def each_other(me, nw, act):
+def each_other(me, nw, act, between=lambda: None):
     if nw != 128:
+        between()
         lax.fori_loop(1, nw, lambda k, carry: (act(lax.rem(me + k, nw)), carry)[1], 0)
         return
     x, z, c = me >> 5, (me >> 1) & 15, me & 1
@@ -49,7 +50,9 @@
             act(plane | there)
         return carry
 
-    lax.fori_loop(0, 15, level, 0)
+    lax.fori_loop(0, 5, level, 0)
+    between()
+    lax.fori_loop(5, 15, level, 0)
     for plane in planes[:-1]:
         act(plane | (z << 1))
 
@@ -72,19 +75,21 @@
     def greet(to):
         pl.semaphore_signal(barrier, inc=1, device_id=(to, y), device_id_type=MESH)
 
-    each_other(me, nw, greet)
-    for k in range(1, ng):
-        pl.semaphore_signal(barrier, inc=1, device_id=(me, lax.rem(y + k, ng)), device_id_type=MESH)
-
     bring = [pltpu.make_async_copy(*pair, in_sem.at[i]) for i, pair in enumerate((
         (bas_hbm, bas_ref), (spec_hbm, spec_ref), (wn_hbm, wn_ref), (blk_hbm, blk_ref),
         (wgt_hbm, wgt_ref)))]
-    for copy in bring[:2]:
-        copy.start()
-    for m in range(mloc):
-        pltpu.make_async_copy(leg_hbm.at[m], leg.at[m], leg_sem.at[m]).start()
-    for copy in bring[2:]:
-        copy.start()
+
+    def load():
+        for copy in bring[:2]:
+            copy.start()
+        for m in range(mloc):
+            pltpu.make_async_copy(leg_hbm.at[m], leg.at[m], leg_sem.at[m]).start()
+        for copy in bring[2:]:
+            copy.start()
+
+    each_other(me, nw, greet, load)
+    for k in range(1, ng):
+        pl.semaphore_signal(barrier, inc=1, device_id=(me, lax.rem(y + k, ng)), device_id_type=MESH)
 
     bring[0].wait()
     bas = bas_ref[...]

time: 42.6 us -> 42.5 us (level)
  no operation moved by 1% of the time
where the time goes in v7:
time: 42.5 us; the launch traced here: 42.3 us
  Pallas kernels  40.4 us (95%)
  local copies, waits for them, and re-layouts  1.27 us (3%)
  between operations  0.64 us (2%)
    pallas_call x1, Pallas kernels, per_device(): pl.pallas_call(functools.partial(kernel, nw, ng), out_shape=(jax.ShapeDty...  40.4 us
    unnamed x2, local copies, waits for them, and re-layouts  1.27 us

profile of v7, /device:TPU:1, one launch (start us, length us, event | category | flops | bytes accessed | tf_op | source)
XLA Modules:
  0.0 42.3 jit_solution(17764680790777920016)
XLA Ops:
  0.6 40.4 %shard_map.77 = (bf16[4,160,128]{2,1,0:T(8,128)(2,1)S(1)}, f32[4,4,128]{2,1,0:T(4,128)S(1)}) custom-call(bf16[4,10,2,1280]{3,2,1,0:T(2,128)(2,1)} %bitcast.13, bf16[10,1280,128]{2,1,0:T(8,128)(2,1)} %leg_hbm.1, s32[10]{0:T(128)} %wn_hbm.1, s32[8,128]{1,0:T(8,128)} %bitcast.14, bf16[1024,128]{1,0:T(8,128)(2,1)} %bitcast.12, s32[8,128]{1,0:T(8,128)} %bitcast.15), custom_call_target="tpu_custom_call" | custom-call | tf_op jit(solution)/shard_map/pallas_call | solution.py:325
  41.1 0.7 %copy.11 = bf16[4,2,1,10240]{3,1,2,0:T(2,128)(2,1)} copy(bf16[4,2,1,10240]{3,1,2,0:T(2,128)(2,1)S(1)} %bitcast.10) | data formatting | bytes 327680
  41.7 0.6 %copy.12 = f32[16,128]{1,0:T(8,128)} copy(f32[16,128]{1,0:T(8,128)S(1)} %bitcast.11) | data formatting | bytes 16384
